TPU v7x, 512 devices: a whole 4x8x8 slice. The times are simulated.
512 devices in a mesh: ta: 8 (over z_hi, core), ha: 8 (over y), wa: 8 (over z_lo, x).
Axes of the slice: x: 4, y: 8, z: 8 (z_hi: 4, z_lo: 2; z = z_hi * 2 + z_lo), core: 2. Of those that a mesh axis runs over, the one named last changes fastest.
Arguments:
- query_tokens: bfloat16 [8, 8, 384, 3072], P('ha', 'wa', 'ta'), may hold values from -5 to 5
- key_tokens: bfloat16 [8, 8, 384, 3072], P('ha', 'wa', 'ta'), may hold values from -5 to 5
- value_tokens: bfloat16 [8, 8, 384, 3072], P('ha', 'wa', 'ta'), may hold values from -5 to 5
- grad_output: bfloat16 [8, 8, 384, 3072], P('ha', 'wa', 'ta'), may hold values from -5 to 5
- windows: int32 [24, 2], replicated, may hold values from 1 to 3, as said below
Outputs:
- grad_queries: bfloat16 [8, 8, 384, 3072], P('ha', 'wa', 'ta')
- grad_keys: bfloat16 [8, 8, 384, 3072], P('ha', 'wa', 'ta')
- grad_values: bfloat16 [8, 8, 384, 3072], P('ha', 'wa', 'ta')
Inputs may be any that keep to these rules, and one draw needn't show every extreme that they name: `windows`: every entry is 1 or 3; some head has 3 along both axes.
All inputs are finite; a program needn't handle non-finite values.
Results may differ from a plain program's by a relative error of at most 0.035.
Values may be sent and summed in bfloat16 or wider, within the bound.
No kernel may reach another device: no remote copies, remote signals or barrier semaphores. Data moves between devices by JAX's collectives and lax.ppermute only.
A program may use at most 128 MiB of HBM per device.

v0:
```python
import functools

import jax
import jax.numpy as jnp
import numpy as np
from jax import lax
from jax.experimental import pallas as pl
from jax.experimental.pallas import tpu as pltpu
from jax.sharding import PartitionSpec as P

head_dim = 128
log2_e = 1.4426950408889634
contract_last = (((1,), (1,)), ((), ()))
small_vmem = 12 * 1024 * 1024
attend_vmem = 44 * 1024 * 1024
hbm_spec = pl.BlockSpec(memory_space=pltpu.HBM)
vmem_spec = pl.BlockSpec(memory_space=pltpu.VMEM)
smem_spec = pl.BlockSpec(memory_space=pltpu.SMEM)
small_params = pltpu.CompilerParams(vmem_limit_bytes=small_vmem)


def pair_partner(kind, index, count):
    partner = index ^ 1 if kind == 1 else ((index + 1) ^ 1) - 1
    return partner if 0 <= partner < count else None


def exchange(value, which, kind):
    parts, rows, cols = (lax.axis_size(name) for name in ("ta", "ha", "wa"))
    pairs = []
    for part in range(parts):
        along_rows = (part % 2 == 0) == (which == 1)
        for row in range(rows):
            for col in range(cols):
                to_row, to_col = row, col
                if along_rows:
                    to_row = pair_partner(kind, row, rows)
                else:
                    to_col = pair_partner(kind, col, cols)
                if to_row is not None and to_col is not None:
                    pairs.append(
                        ((part * rows + row) * cols + col, (part * rows + to_row) * cols + to_col)
                    )
    return lax.ppermute(value, ("ta", "ha", "wa"), pairs)


def unpack_kernel(order, packed, *targets):
    devices, slots = packed.shape[:2]
    for rank in range(devices * slots):
        column = pl.multiple_of(order[rank] * head_dim, head_dim)
        for place, target in enumerate(targets):
            target[:, pl.ds(column, head_dim)] = packed[rank % devices, rank // devices, place]


def unpack(order, packed):
    devices, slots, count, tokens, _ = packed.shape
    flat = jax.ShapeDtypeStruct((tokens, devices * slots * head_dim), packed.dtype)
    return pl.pallas_call(
        unpack_kernel,
        out_shape=[flat] * count,
        in_specs=[smem_spec, vmem_spec],
        compiler_params=small_params,
    )(order, packed)


def attend_kernel(full, valid, *refs):
    qg_in, own_in, first_in, second_in = refs[0], refs[1], refs[2:4], refs[4:6]
    dq_out, own_out, first_out, second_out = refs[6], refs[7], refs[8:10], refs[10:12]
    (qg, kv, score, dprob, part, dq, top, total, weighted, dq_t, load_sem, store_sem) = refs[12:]
    chunks, slots, _, rows, _ = qg.shape
    tile = chunks * rows
    scale = head_dim ** (-0.5)
    to_log2 = scale * log2_e
    head = pl.ds(0, full)
    tail = pl.ds(full, slots - full)

    def relayed(b):
        return pl.ds(slots + b * full, full)

    early = [(qg_in, qg), (own_in, kv.at[0])]
    early += [(first_in[a].at[:, pl.ds(0, slots)], kv.at[a + 1]) for a in range(2)]
    late = []
    for b in range(2):
        late.append((second_in[b], kv.at[3 * b + 3, :, head]))
        late += [
            (first_in[a].at[:, relayed(b)], kv.at[3 * b + 4 + a, :, head]) for a in range(2)
        ]
    early = [pltpu.make_async_copy(*pair, load_sem.at[n]) for n, pair in enumerate(early)]
    late = [
        pltpu.make_async_copy(*pair, load_sem.at[len(early) + n]) for n, pair in enumerate(late)
    ]
    for copy in early + late:
        copy.start()

    def over_rows(slot, lines, step):
        def one_line(line, carry):
            start = 3 * line
            here = [valid[slot, start + a] for a in range(3)]
            whole = here[0] * here[1] * here[2]

            @pl.when(whole != 0)
            def _():
                step(start, 3)

            @pl.when(whole == 0)
            def _():
                def one_place(a, carry):
                    @pl.when(valid[slot, start + a] != 0)
                    def _():
                        step(start + a, 1)

                    return carry

                lax.fori_loop(0, 3, one_place, 0)

            return carry

        lax.fori_loop(0, lines, one_line, 0)

    def one_slot(slot, lines):
        query = qg[:, slot, 0].reshape(tile, head_dim)
        grad = qg[:, slot, 1].reshape(tile, head_dim)
        top[...] = jnp.full(top.shape, -1e30, jnp.float32)
        total[...] = jnp.zeros(total.shape, jnp.float32)
        weighted[...] = jnp.zeros(weighted.shape, jnp.float32)
        dq_t[...] = jnp.zeros(dq_t.shape, jnp.float32)

        def forward(start, count):
            near = pl.ds(start, count)
            key = kv[near, :, slot, 0].reshape(count * tile, head_dim)
            value = kv[near, :, slot, 1].reshape(count * tile, head_dim)
            raw = lax.dot_general(key, query, contract_last, preferred_element_type=jnp.float32)
            rise = lax.dot_general(value, grad, contract_last, preferred_element_type=jnp.float32)
            score[near] = raw.reshape(count, tile, tile)
            dprob[near] = rise.reshape(count, tile, tile)
            top_old = top[...]
            top_new = jnp.maximum(top_old, jnp.max(raw, axis=0, keepdims=True))
            fade = jnp.exp2((top_old - top_new) * to_log2)
            spread = jnp.exp2((raw - top_new) * to_log2)
            top[...] = top_new
            total[...] = total[...] * fade + jnp.sum(spread, axis=0, keepdims=True)
            weighted[...] = weighted[...] * fade + jnp.sum(spread * rise, axis=0, keepdims=True)

        over_rows(slot, lines, forward)
        log_total = top[...] * to_log2 + jnp.log(total[...]) * log2_e
        delta = weighted[...] / total[...]

        def backward(start, count):
            near = pl.ds(start, count)
            key = kv[near, :, slot, 0].reshape(count * tile, head_dim)
            raw = score[near].reshape(count * tile, tile)
            rise = dprob[near].reshape(count * tile, tile)
            prob = jnp.exp2(raw * to_log2 - log_total)
            weight = prob.astype(jnp.bfloat16)
            dscore = (prob * (rise - delta)).astype(jnp.bfloat16)
            dv = jnp.dot(weight, grad, preferred_element_type=jnp.float32)
            dk = jnp.dot(dscore, query, preferred_element_type=jnp.float32) * scale
            dq_t[...] += jnp.dot(key.T, dscore, preferred_element_type=jnp.float32)
            shape = (count, chunks, rows, head_dim)
            part[near, :, slot, 0] = dk.astype(jnp.bfloat16).reshape(shape)
            part[near, :, slot, 1] = dv.astype(jnp.bfloat16).reshape(shape)

        over_rows(slot, lines, backward)
        dq_here = (dq_t[...] * scale).T.astype(jnp.bfloat16)
        dq[:, slot, 0] = dq_here.reshape(chunks, rows, head_dim)

    def tail_slot(slot, carry):
        one_slot(slot, 1)
        return carry

    def full_slot(slot, carry):
        one_slot(slot, 3)
        return carry

    def store(pairs, base):
        copies = [
            pltpu.make_async_copy(*pair, store_sem.at[base + n]) for n, pair in enumerate(pairs)
        ]
        for copy in copies:
            copy.start()
        return copies

    for copy in early:
        copy.wait()
    stores = []
    if full < slots:
        lax.fori_loop(full, slots, tail_slot, 0)
        pairs = [(part.at[0, :, tail], own_out.at[:, tail])]
        pairs += [(part.at[a + 1, :, tail], first_out[a].at[:, tail]) for a in range(2)]
        stores += store(pairs, 0)
    for copy in late:
        copy.wait()
    lax.fori_loop(0, full, full_slot, 0)
    pairs = []
    for a in range(2):
        pairs.append((part.at[a + 1, :, head], first_out[a].at[:, head]))
        pairs += [
            (part.at[3 * b + 4 + a, :, head], first_out[a].at[:, relayed(b)]) for b in range(2)
        ]
    pairs += [(part.at[3 * b + 3, :, head], second_out[b]) for b in range(2)]
    pairs += [(part.at[0, :, head], own_out.at[:, head]), (dq, dq_out)]
    stores += store(pairs, 3)
    for copy in stores:
        copy.wait()


def attend(valid, qg, own, first, second, full):
    chunks, slots, _, rows, _ = qg.shape
    tile = chunks * rows
    bf16, f32 = jnp.bfloat16, jnp.float32
    units = 9 * full + 3 * (slots - full)
    near = [own, *first, *second]
    dq_shape = (chunks, slots, 1, rows, head_dim)
    outs = pl.pallas_call(
        functools.partial(attend_kernel, full),
        out_shape=[jax.ShapeDtypeStruct(dq_shape, bf16)]
        + [jax.ShapeDtypeStruct(array.shape, bf16) for array in near],
        in_specs=[smem_spec] + [hbm_spec] * 6,
        out_specs=[hbm_spec] * 6,
        scratch_shapes=[
            pltpu.VMEM(qg.shape, bf16),
            pltpu.VMEM((9,) + own.shape, bf16),
            pltpu.VMEM((9, tile, tile), f32),
            pltpu.VMEM((9, tile, tile), f32),
            pltpu.VMEM((9,) + own.shape, bf16),
            pltpu.VMEM(dq_shape, bf16),
            pltpu.VMEM((1, tile), f32),
            pltpu.VMEM((1, tile), f32),
            pltpu.VMEM((1, tile), f32),
            pltpu.VMEM((head_dim, tile), f32),
            pltpu.SemaphoreType.DMA((10,)),
            pltpu.SemaphoreType.DMA((13,)),
        ],
        compiler_params=pltpu.CompilerParams(vmem_limit_bytes=attend_vmem),
        cost_estimate=pl.CostEstimate(
            flops=units * 10 * tile * tile * head_dim,
            bytes_accessed=8 * 1024 * 1024,
            transcendentals=units * 2 * tile * tile,
        ),
    )(valid, qg, *near)
    return outs[0], outs[1], outs[2:4], outs[4:6]


def relay_kernel(valid, *refs):
    second, first, out = refs[0:2], refs[2:4], refs[4:6]
    full = out[0].shape[1]
    slots = first[0].shape[1] - 2 * full
    for b in range(2):
        for slot in range(full):
            total = second[b][:, slot].astype(jnp.float32)
            for a in range(2):
                arrived = first[a][:, slots + b * full + slot].astype(jnp.float32)
                total += jnp.where(valid[slot, 3 * b + 4 + a] != 0, arrived, 0.0)
            out[b][:, slot] = total.astype(out[b].dtype)


def relay(valid, second, first):
    return pl.pallas_call(
        relay_kernel,
        out_shape=[jax.ShapeDtypeStruct(array.shape, array.dtype) for array in second],
        in_specs=[smem_spec] + [vmem_spec] * 4,
        compiler_params=small_params,
    )(valid, *second, *first)


def combine_kernel(valid, own, *refs):
    first, second, out = refs[0:2], refs[2:4], refs[4]
    full = second[0].shape[1]
    for slot in range(out.shape[1]):
        total = own[:, slot].astype(jnp.float32)
        for a in range(2):
            arrived = first[a][:, slot].astype(jnp.float32)
            total += jnp.where(valid[slot, a + 1] != 0, arrived, 0.0)
        if slot < full:
            for b in range(2):
                arrived = second[b][:, slot].astype(jnp.float32)
                total += jnp.where(valid[slot, 3 * b + 3] != 0, arrived, 0.0)
        out[:, slot] = total.astype(out.dtype)


def combine(valid, own, first, second):
    return pl.pallas_call(
        combine_kernel,
        out_shape=jax.ShapeDtypeStruct(own.shape, own.dtype),
        in_specs=[smem_spec] + [vmem_spec] * 5,
        compiler_params=small_params,
    )(valid, own, *first, *second)


def swap(blocks):
    return lax.all_to_all(blocks, "ta", split_axis=0, concat_axis=0, tiled=True)


def with_corners(full, order, valid, kv, qg):
    kv_full = lax.slice_in_dim(kv, 0, full, axis=1)
    second = [exchange(kv_full, 2, kind) for kind in (1, 2)]
    qg, second[0] = lax.optimization_barrier((qg, second[0]))
    qg = swap(qg)
    message = jnp.concatenate([kv, *second], axis=1)
    first = [exchange(message, 1, kind) for kind in (1, 2)]
    dq, own, first, second = attend(valid, qg, kv, first, second, full)
    first = [exchange(first[kind - 1], 1, kind) for kind in (1, 2)]
    dq = swap(dq)
    second = relay(valid, second, first)
    second = [exchange(second[kind - 1], 2, kind) for kind in (1, 2)]
    dkv = swap(combine(valid, own, first, second))
    return tuple(unpack(order, dq) + unpack(order, dkv))


def place_heads(devices, shape, windows, order, valid, choice):
    heads = windows.shape[0]
    slots, half = heads // devices, devices // 2
    kinds = []
    for head in range(heads):
        tall = lax.shift_right_logical(windows[head, 0] - 1, 1)
        wide = lax.shift_right_logical(windows[head, 1] - 1, 1)
        kinds.append(2 * tall + wide)

    def count(kind):
        return functools.reduce(
            lambda a, b: a + b, [(other == kind).astype(jnp.int32) for other in kinds]
        )

    both, rows_only, cols_only = count(3), count(2), count(1)

    def over(count, room):
        return jnp.maximum(count - room, 0)

    chosen = jnp.int32(slots - 1)
    for full in range(slots - 1, 0, -1):
        room = half * (slots - full)
        needed = both + over(rows_only, room) + over(cols_only, room)
        chosen = jnp.where(needed <= devices * full, full - 1, chosen)
    choice[0] = chosen
    full = chosen + 1
    room = half * (slots - full)
    used = both + over(rows_only, room) + over(cols_only, room)
    free = devices * full - used
    rows_used, cols_used = jnp.minimum(rows_only, room), jnp.minimum(cols_only, room)
    rows_free = room - rows_used

    def single(nth, odd):
        return devices * full + devices * lax.div(nth, half) + 2 * lax.rem(nth, half) + odd

    seen = [jnp.int32(0)] * 4
    for head in range(heads):
        kind = kinds[head]
        at = [None] * 4
        at[3] = seen[3]
        at[2] = jnp.where(seen[2] < room, single(seen[2], 0), both + seen[2] - room)
        at[1] = jnp.where(
            seen[1] < room,
            single(seen[1], 1),
            both + over(rows_only, room) + seen[1] - room,
        )
        at[0] = jnp.where(
            seen[0] < free,
            used + seen[0],
            jnp.where(
                seen[0] < free + rows_free,
                single(rows_used + seen[0] - free, 0),
                single(cols_used + seen[0] - free - rows_free, 1),
            ),
        )
        place = at[0]
        for other in range(1, 4):
            place = jnp.where(kind == other, at[other], place)
        order[place] = jnp.int32(head)
        for other in range(4):
            seen[other] = seen[other] + (kind == other).astype(jnp.int32)

    part, row, col = (lax.axis_index(name) for name in ("ta", "ha", "wa"))
    by_rows = lax.rem(part, 2) == 0

    def inside(kind, index, count):
        if kind == 0:
            return jnp.int32(1)
        partner = index ^ 1 if kind == 1 else ((index + 1) ^ 1) - 1
        return ((partner >= 0) & (partner < count)).astype(jnp.int32)

    in_rows = [inside(kind, row, shape[0]) for kind in range(3)]
    in_cols = [inside(kind, col, shape[1]) for kind in range(3)]
    for slot in range(slots):
        head = order[slot * devices + part]
        tall = lax.shift_right_logical(windows[head, 0] - 1, 1)
        wide = lax.shift_right_logical(windows[head, 1] - 1, 1)
        along_rows = [in_rows[0], in_rows[1] * tall, in_rows[2] * tall]
        along_cols = [in_cols[0], in_cols[1] * wide, in_cols[2] * wide]
        for b in range(3):
            for a in range(3):
                valid[slot, 3 * b + a] = jnp.where(
                    by_rows, along_rows[a] * along_cols[b], along_cols[a] * along_rows[b]
                )


def prepare_kernel(shape, windows, *refs):
    sources, (order, valid, choice, kv, qg) = refs[:4], refs[4:]
    devices, slots = kv.shape[:2]
    place_heads(devices, shape, windows, order, valid, choice)
    for rank in range(devices * slots):
        column = pl.multiple_of(order[rank] * head_dim, head_dim)
        for n, source in enumerate(sources):
            packed = kv if n < 2 else qg
            packed[rank % devices, rank // devices, n % 2] = source[:, pl.ds(column, head_dim)]


def on_device(query_tokens, key_tokens, value_tokens, grad_output, windows):
    devices = lax.axis_size("ta")
    heads = windows.shape[0]
    slots = heads // devices
    tokens, features = query_tokens.shape[-2:]
    block = jax.ShapeDtypeStruct((devices, slots, 2, tokens, head_dim), query_tokens.dtype)
    arrays = (key_tokens, value_tokens, query_tokens, grad_output)
    shape = (lax.axis_size("ha"), lax.axis_size("wa"))
    order, valid, choice, kv, qg = pl.pallas_call(
        functools.partial(prepare_kernel, shape),
        out_shape=[
            jax.ShapeDtypeStruct((heads,), jnp.int32),
            jax.ShapeDtypeStruct((slots, 9), jnp.int32),
            jax.ShapeDtypeStruct((1,), jnp.int32),
            block,
            block,
        ],
        in_specs=[smem_spec] + [vmem_spec] * 4,
        out_specs=[smem_spec] * 3 + [vmem_spec] * 2,
        compiler_params=small_params,
    )(windows, *[array.reshape(tokens, features) for array in arrays])
    kv = swap(kv)
    branches = [functools.partial(with_corners, full) for full in range(1, slots + 1)]
    outs = lax.switch(choice[0], branches, order, valid, kv, qg)
    return tuple(out.reshape(query_tokens.shape) for out in outs)


def solution(mesh):
    shares = P("ha", "wa", "ta", None)
    return jax.shard_map(
        on_device,
        mesh=mesh,
        in_specs=(shares, shares, shares, shares, P()),
        out_specs=(shares, shares, shares),
        check_vma=False,
    )
```

profile of v0, /device:TPU:89, one launch (start us, length us, event | category | flops | bytes accessed | tf_op | source)
XLA Modules:
  0.0 149.2 jit_solution(7650107881027986302)
XLA Ops:
  0.6 0.8 copy.8.windows
  1.4 1.0 copy-done.9
  2.4 1.0 copy-done.10
  3.3 1.0 copy-done.11
  4.3 1.0 copy-done.12
  5.2 2.8 %shard_map.76 = (s32[24]{0:T(128)S(1)}, s32[3,9]{1,0:T(4,128)S(1)}, s32[1]{0:T(128)}, bf16[8,3,2,48,128]{4,3,2,1,0:T(8,128)(2,1)}, bf16[8,3,2,48,128]{4,3,2,1,0:T(8,128)(2,1)}) custom-call(s32[24,2]{1,0:T(8,128)S(1)} %copy.8.windows, bf16[48,3072]{1,0:T(8,128)(2,1)S(1)} %bitcast.10, bf16[48,3072]{1,0:T(8,128)(2,1)S(1)} %bitcast.11, ...), custom_call_target="tpu_custom_call" | custom-call | tf_op jit(solution)/shard_map/pallas_call | solution.py:414
  8.1 10.1 %all-to-all-start.9 = ((bf16[8,3,2,48,128]{4,3,2,1,0:T(8,128)(2,1)}), bf16[8,3,2,48,128]{4,3,2,1,0:T(8,128)(2,1)S(1)}, u32[]{:S(2)}, u32[]{:S(2)}) async-start(bf16[8,3,2,48,128]{4,3,2,1,0:T(8,128)(2,1)} %get-tuple-element.85), calls=%async_computation.9 | async-start | bytes 1179648 | tf_op jit(solution)/shard_map/all_to_all | solution.py:290
  18.8 17.6 %all-to-all-done.9 = bf16[8,3,2,48,128]{4,3,2,1,0:T(8,128)(2,1)S(1)} async-done(((bf16[8,3,2,48,128]{4,3,2,1,0:T(8,128)(2,1)}), bf16[8,3,2,48,128]{4,3,2,1,0:T(8,128)(2,1)S(1)}, u32[]{:S(2)}, u32[]{:S(2)}) %all-to-all-start.9) | async-done | bytes 589856 | tf_op jit(solution)/shard_map/all_to_all | solution.py:290
  36.4 112.0 %conditional.1 = (bf16[48,3072]{1,0:T(8,128)(2,1)}, bf16[48,3072]{1,0:T(8,128)(2,1)}, bf16[1,1,48,3072]{3,2,1,0:T(8,128)(2,1)S(1)}) conditional(s32[]{:T(128)} %bitcast.7, (bf16[8,3,2,48,128]{4,3,2,1,0:T(8,128)(2,1)S(1)}, bf16[8,3,2,48,128]{4,3,2,1,0:T(8,128)(2,1)}, s32[3,9]{1,0:T(4,128)S(1)}, s32[24]{0:T(128)S(1)}) %tuple.26, ...), branch_computations={%region_0.0_spmd, %region_1.0_spmd, %region_2.0_spmd} | conditional | flops 5096079360 | bytes 68846112 | solution.py:429
  36.4 2.1 %collective-permute-start = (bf16[8,1,2,48,128]{4,3,2,1,0:T(8,128)(2,1)S(1)}, bf16[8,1,2,48,128]{4,3,2,1,0:T(8,128)(2,1)S(1)}, u32[]{:S(2)}, u32[]{:S(2)}) collective-permute-start(bf16[8,1,2,48,128]{4,3,2,1,0:T(8,128)(2,1)S(1)} %slice.4), channel_id=1, source_target_pairs={{0,1},{1,0},{2,3},{3,2},{4,5},{5,4},{6,7},{7,6},{8,9},{9,8},{10,11... | collective-permute-start | bytes 589832 | tf_op jit(solution)/shard_map/cond/branch_0_fun/ppermute | solution.py:43
  38.5 4.6 %collective-permute-start.1 = (bf16[8,1,2,48,128]{4,3,2,1,0:T(8,128)(2,1)S(1)}, bf16[8,1,2,48,128]{4,3,2,1,0:T(8,128)(2,1)S(1)}, u32[]{:S(2)}, u32[]{:S(2)}) collective-permute-start(bf16[8,1,2,48,128]{4,3,2,1,0:T(8,128)(2,1)S(1)} %slice.4), channel_id=1, source_target_pairs={{1,2},{2,1},{3,4},{4,3},{5,6},{6,5},{9,10},{10,9},{11,12},{12,11},... | collective-permute-start | bytes 589832 | tf_op jit(solution)/shard_map/cond/branch_0_fun/ppermute | solution.py:43
  43.2 5.6 %all-to-all-start = ((bf16[8,3,2,48,128]{4,3,2,1,0:T(8,128)(2,1)}), bf16[8,3,2,48,128]{4,3,2,1,0:T(8,128)(2,1)S(1)}, u32[]{:S(2)}, u32[]{:S(2)}) async-start(bf16[8,3,2,48,128]{4,3,2,1,0:T(8,128)(2,1)} %get-tuple-element.29), calls=%async_computation | async-start | bytes 1179648 | tf_op jit(solution)/shard_map/cond/branch_0_fun/all_to_all | solution.py:290
  49.0 4.5 %collective-permute-start.3 = (bf16[8,5,2,48,128]{4,3,2,1,0:T(8,128)(2,1)S(1)}, bf16[8,5,2,48,128]{4,3,2,1,0:T(8,128)(2,1)S(1)}, u32[]{:S(2)}, u32[]{:S(2)}) collective-permute-start(bf16[8,5,2,48,128]{4,3,2,1,0:T(8,128)(2,1)S(1)} %constant_dynamic-update-slice_fusion), channel_id=1, source_target_pairs={{8,16},{9,17},{10,18},{11,19},{12,20},{13,21},{14,22},{15,23},{16,... | collective-permute-start | bytes 2949128 | tf_op jit(solution)/shard_map/cond/branch_0_fun/ppermute | solution.py:43
  53.4 1.9 %collective-permute-start.2 = (bf16[8,5,2,48,128]{4,3,2,1,0:T(8,128)(2,1)S(1)}, bf16[8,5,2,48,128]{4,3,2,1,0:T(8,128)(2,1)S(1)}, u32[]{:S(2)}, u32[]{:S(2)}) collective-permute-start(bf16[8,5,2,48,128]{4,3,2,1,0:T(8,128)(2,1)S(1)} %constant_dynamic-update-slice_fusion), channel_id=1, source_target_pairs={{0,8},{1,9},{2,10},{3,11},{4,12},{5,13},{6,14},{7,15},{8,0},{9,1},... | collective-permute-start | bytes 2949128 | tf_op jit(solution)/shard_map/cond/branch_0_fun/ppermute | solution.py:43
  55.4 20.4 %collective-permute-done.3.refs_3_ = bf16[8,5,2,48,128]{4,3,2,1,0:T(8,128)(2,1)S(1)} collective-permute-done((bf16[8,5,2,48,128]{4,3,2,1,0:T(8,128)(2,1)S(1)}, bf16[8,5,2,48,128]{4,3,2,1,0:T(8,128)(2,1)S(1)}, u32[]{:S(2)}, u32[]{:S(2)}) %collective-permute-start.3) | collective-permute-done | bytes 983072 | tf_op jit(solution)/shard_map/cond/branch_0_fun/ppermute | solution.py:43
  75.8 1.0 copy-done.13
  76.8 1.2 copy-done.14
  78.0 11.8 %branch_0_fun.5 = (bf16[8,3,1,48,128]{4,3,2,1,0:T(8,128)(2,1)}, bf16[8,3,2,48,128]{4,3,2,1,0:T(8,128)(2,1)S(1)}, bf16[8,5,2,48,128]{4,3,2,1,0:T(8,128)(2,1)}, bf...) custom-call(s32[3,9]{1,0:T(4,128)S(1)} %get-tuple-element.26.valid, ...), custom_call_target="tpu_custom_call" | custom-call | flops 2831155200 | bytes 8388608 | tf_op jit(solution)/shard_map/cond/branch_0_fun/pallas_call | solution.py:213
  89.9 1.9 %collective-permute-start.4 = (bf16[8,5,2,48,128]{4,3,2,1,0:T(8,128)(2,1)}, bf16[8,5,2,48,128]{4,3,2,1,0:T(8,128)(2,1)S(1)}, u32[]{:S(2)}, u32[]{:S(2)}) collective-permute-start(bf16[8,5,2,48,128]{4,3,2,1,0:T(8,128)(2,1)} %get-tuple-element.32), channel_id=1, source_target_pairs={{0,8},{1,9},{2,10},{3,11},{4,12},{5,13},{6,14},{7,15},{8,0},{9,1},... | collective-permute-start | bytes 2949128 | tf_op jit(solution)/shard_map/cond/branch_0_fun/ppermute | solution.py:43
  91.8 2.9 %collective-permute-start.5 = (bf16[8,5,2,48,128]{4,3,2,1,0:T(8,128)(2,1)}, bf16[8,5,2,48,128]{4,3,2,1,0:T(8,128)(2,1)S(1)}, u32[]{:S(2)}, u32[]{:S(2)}) collective-permute-start(bf16[8,5,2,48,128]{4,3,2,1,0:T(8,128)(2,1)} %get-tuple-element.33), channel_id=1, source_target_pairs={{8,16},{9,17},{10,18},{11,19},{12,20},{13,21},{14,22},{15,23},{16,... | collective-permute-start | bytes 2949128 | tf_op jit(solution)/shard_map/cond/branch_0_fun/ppermute | solution.py:43
  94.7 6.3 %all-to-all-start.2 = ((bf16[8,3,1,48,128]{4,3,2,1,0:T(8,128)(2,1)}), bf16[8,3,1,48,128]{4,3,2,1,0:T(8,128)(2,1)S(1)}, u32[]{:S(2)}, u32[]{:S(2)}) async-start(bf16[8,3,1,48,128]{4,3,2,1,0:T(8,128)(2,1)} %get-tuple-element.40), calls=%async_computation.2 | async-start | bytes 589824 | tf_op jit(solution)/shard_map/cond/branch_0_fun/all_to_all | solution.py:290
  101.0 3.9 %collective-permute-done.4.refs_2_.refs_0_ = bf16[8,5,2,48,128]{4,3,2,1,0:T(8,128)(2,1)S(1)} collective-permute-done((bf16[8,5,2,48,128]{4,3,2,1,0:T(8,128)(2,1)}, bf16[8,5,2,48,128]{4,3,2,1,0:T(8,128)(2,1)S(1)}, u32[]{:S(2)}, u32[]{:S(2)}) %collective-permute-start.4) | collective-permute-done | bytes 983072 | tf_op jit(solution)/shard_map/cond/branch_0_fun/ppermute | solution.py:43
  104.9 8.8 %collective-permute-done.5.refs_3_.refs_1_ = bf16[8,5,2,48,128]{4,3,2,1,0:T(8,128)(2,1)S(1)} collective-permute-done((bf16[8,5,2,48,128]{4,3,2,1,0:T(8,128)(2,1)}, bf16[8,5,2,48,128]{4,3,2,1,0:T(8,128)(2,1)S(1)}, u32[]{:S(2)}, u32[]{:S(2)}) %collective-permute-start.5) | collective-permute-done | bytes 983072 | tf_op jit(solution)/shard_map/cond/branch_0_fun/ppermute | solution.py:43
  113.7 0.8 branch_0_fun.6
  114.5 2.1 %collective-permute-start.6 = (bf16[8,1,2,48,128]{4,3,2,1,0:T(8,128)(2,1)S(1)}, bf16[8,1,2,48,128]{4,3,2,1,0:T(8,128)(2,1)S(1)}, u32[]{:S(2)}, u32[]{:S(2)}) collective-permute-start(bf16[8,1,2,48,128]{4,3,2,1,0:T(8,128)(2,1)S(1)} %get-tuple-element.36), channel_id=1, source_target_pairs={{0,1},{1,0},{2,3},{3,2},{4,5},{5,4},{6,7},{7,6},{8,9},{9,8},{10,11... | collective-permute-start | bytes 589832 | tf_op jit(solution)/shard_map/cond/branch_0_fun/ppermute | solution.py:43
  116.6 5.7 %collective-permute-start.7 = (bf16[8,1,2,48,128]{4,3,2,1,0:T(8,128)(2,1)S(1)}, bf16[8,1,2,48,128]{4,3,2,1,0:T(8,128)(2,1)S(1)}, u32[]{:S(2)}, u32[]{:S(2)}) collective-permute-start(bf16[8,1,2,48,128]{4,3,2,1,0:T(8,128)(2,1)S(1)} %get-tuple-element.37), channel_id=1, source_target_pairs={{1,2},{2,1},{3,4},{4,3},{5,6},{6,5},{9,10},{10,9},{11,12},{12,11},... | collective-permute-start | bytes 589832 | tf_op jit(solution)/shard_map/cond/branch_0_fun/ppermute | solution.py:43
  122.3 3.0 %collective-permute-done.7.refs_3_ = bf16[8,1,2,48,128]{4,3,2,1,0:T(8,128)(2,1)S(1)} collective-permute-done((bf16[8,1,2,48,128]{4,3,2,1,0:T(8,128)(2,1)S(1)}, bf16[8,1,2,48,128]{4,3,2,1,0:T(8,128)(2,1)S(1)}, u32[]{:S(2)}, u32[]{:S(2)}) %collective-permute-start.7) | collective-permute-done | bytes 196640 | tf_op jit(solution)/shard_map/cond/branch_0_fun/ppermute | solution.py:43
  125.3 1.8 %branch_0_fun.7 = bf16[8,3,2,48,128]{4,3,2,1,0:T(8,128)(2,1)} custom-call(s32[3,9]{1,0:T(4,128)S(1)} %get-tuple-element.26.valid, bf16[8,3,2,48,128]{4,3,2,1,0:T(8,128)(2,1)S(1)} %get-tuple-element.31.own, bf16[8,5,2,48,128]{4,3,2,1,0:T(8,128)(2,1)S(1)} %collective-permute-done.4.refs_2_.refs_0_, ...), custom_call_target="tpu_custom_call" | custom-call | tf_op jit(solution)/shard_map/cond/branch_0_fun/pallas_call | solution.py:281
  127.1 3.9 %all-to-all-start.1 = ((bf16[8,3,2,48,128]{4,3,2,1,0:T(8,128)(2,1)}), bf16[8,3,2,48,128]{4,3,2,1,0:T(8,128)(2,1)S(1)}, u32[]{:S(2)}, u32[]{:S(2)}) async-start(bf16[8,3,2,48,128]{4,3,2,1,0:T(8,128)(2,1)} %branch_0_fun.7), calls=%async_computation.1 | async-start | bytes 1179648 | tf_op jit(solution)/shard_map/cond/branch_0_fun/all_to_all | solution.py:290
  131.6 15.3 %all-to-all-done.1.packed = bf16[8,3,2,48,128]{4,3,2,1,0:T(8,128)(2,1)S(1)} async-done(((bf16[8,3,2,48,128]{4,3,2,1,0:T(8,128)(2,1)}), bf16[8,3,2,48,128]{4,3,2,1,0:T(8,128)(2,1)S(1)}, u32[]{:S(2)}, u32[]{:S(2)}) %all-to-all-start.1) | async-done | bytes 589856 | tf_op jit(solution)/shard_map/cond/branch_0_fun/all_to_all | solution.py:290
  147.0 1.5 branch_0_fun.8
  148.4 0.7 copy-done.16
  (20 shorter events, 0.7 us)
Async XLA Ops:
  1.4 1.0 copy-start.9
  2.4 1.0 copy-start.10
  3.3 1.0 copy-start.11
  4.3 1.0 copy-start.12
  8.1 28.4 %all-to-all-start.9 = ((bf16[8,3,2,48,128]{4,3,2,1,0:T(8,128)(2,1)}), bf16[8,3,2,48,128]{4,3,2,1,0:T(8,128)(2,1)S(1)}, u32[]{:S(2)}, u32[]{:S(2)}) async-start(bf16[8,3,2,48,128]{4,3,2,1,0:T(8,128)(2,1)} %get-tuple-element.85), calls=%async_computation.9 | async-start | bytes 1179648 | tf_op jit(solution)/shard_map/all_to_all | solution.py:290
  36.4 12.5 %copy-start.15 = (bf16[8,3,2,48,128]{4,3,2,1,0:T(8,128)(2,1)}, bf16[8,3,2,48,128]{4,3,2,1,0:T(8,128)(2,1)S(1)}, u32[]{:S(2)}) copy-start(bf16[8,3,2,48,128]{4,3,2,1,0:T(8,128)(2,1)S(1)} %get-tuple-element.28.refs_1_) | copy-start | bytes 1769476 | tf_op jit(solution)/shard_map/cond
  36.4 6.8 %collective-permute-start = (bf16[8,1,2,48,128]{4,3,2,1,0:T(8,128)(2,1)S(1)}, bf16[8,1,2,48,128]{4,3,2,1,0:T(8,128)(2,1)S(1)}, u32[]{:S(2)}, u32[]{:S(2)}) collective-permute-start(bf16[8,1,2,48,128]{4,3,2,1,0:T(8,128)(2,1)S(1)} %slice.4), channel_id=1, source_target_pairs={{0,1},{1,0},{2,3},{3,2},{4,5},{5,4},{6,7},{7,6},{8,9},{9,8},{10,11... | collective-permute-start | bytes 589832 | tf_op jit(solution)/shard_map/cond/branch_0_fun/ppermute | solution.py:43
  38.5 10.4 %collective-permute-start.1 = (bf16[8,1,2,48,128]{4,3,2,1,0:T(8,128)(2,1)S(1)}, bf16[8,1,2,48,128]{4,3,2,1,0:T(8,128)(2,1)S(1)}, u32[]{:S(2)}, u32[]{:S(2)}) collective-permute-start(bf16[8,1,2,48,128]{4,3,2,1,0:T(8,128)(2,1)S(1)} %slice.4), channel_id=1, source_target_pairs={{1,2},{2,1},{3,4},{4,3},{5,6},{6,5},{9,10},{10,9},{11,12},{12,11},... | collective-permute-start | bytes 589832 | tf_op jit(solution)/shard_map/cond/branch_0_fun/ppermute | solution.py:43
  43.2 33.6 %all-to-all-start = ((bf16[8,3,2,48,128]{4,3,2,1,0:T(8,128)(2,1)}), bf16[8,3,2,48,128]{4,3,2,1,0:T(8,128)(2,1)S(1)}, u32[]{:S(2)}, u32[]{:S(2)}) async-start(bf16[8,3,2,48,128]{4,3,2,1,0:T(8,128)(2,1)} %get-tuple-element.29), calls=%async_computation | async-start | bytes 1179648 | tf_op jit(solution)/shard_map/cond/branch_0_fun/all_to_all | solution.py:290
  49.0 26.8 %collective-permute-start.3 = (bf16[8,5,2,48,128]{4,3,2,1,0:T(8,128)(2,1)S(1)}, bf16[8,5,2,48,128]{4,3,2,1,0:T(8,128)(2,1)S(1)}, u32[]{:S(2)}, u32[]{:S(2)}) collective-permute-start(bf16[8,5,2,48,128]{4,3,2,1,0:T(8,128)(2,1)S(1)} %constant_dynamic-update-slice_fusion), channel_id=1, source_target_pairs={{8,16},{9,17},{10,18},{11,19},{12,20},{13,21},{14,22},{15,23},{16,... | collective-permute-start | bytes 2949128 | tf_op jit(solution)/shard_map/cond/branch_0_fun/ppermute | solution.py:43
  53.4 22.4 %collective-permute-start.2 = (bf16[8,5,2,48,128]{4,3,2,1,0:T(8,128)(2,1)S(1)}, bf16[8,5,2,48,128]{4,3,2,1,0:T(8,128)(2,1)S(1)}, u32[]{:S(2)}, u32[]{:S(2)}) collective-permute-start(bf16[8,5,2,48,128]{4,3,2,1,0:T(8,128)(2,1)S(1)} %constant_dynamic-update-slice_fusion), channel_id=1, source_target_pairs={{0,8},{1,9},{2,10},{3,11},{4,12},{5,13},{6,14},{7,15},{8,0},{9,1},... | collective-permute-start | bytes 2949128 | tf_op jit(solution)/shard_map/cond/branch_0_fun/ppermute | solution.py:43
  75.8 1.0 copy-start.13
  76.8 1.2 copy-start.14
  89.9 15.1 %collective-permute-start.4 = (bf16[8,5,2,48,128]{4,3,2,1,0:T(8,128)(2,1)}, bf16[8,5,2,48,128]{4,3,2,1,0:T(8,128)(2,1)S(1)}, u32[]{:S(2)}, u32[]{:S(2)}) collective-permute-start(bf16[8,5,2,48,128]{4,3,2,1,0:T(8,128)(2,1)} %get-tuple-element.32), channel_id=1, source_target_pairs={{0,8},{1,9},{2,10},{3,11},{4,12},{5,13},{6,14},{7,15},{8,0},{9,1},... | collective-permute-start | bytes 2949128 | tf_op jit(solution)/shard_map/cond/branch_0_fun/ppermute | solution.py:43
  91.8 21.9 %collective-permute-start.5 = (bf16[8,5,2,48,128]{4,3,2,1,0:T(8,128)(2,1)}, bf16[8,5,2,48,128]{4,3,2,1,0:T(8,128)(2,1)S(1)}, u32[]{:S(2)}, u32[]{:S(2)}) collective-permute-start(bf16[8,5,2,48,128]{4,3,2,1,0:T(8,128)(2,1)} %get-tuple-element.33), channel_id=1, source_target_pairs={{8,16},{9,17},{10,18},{11,19},{12,20},{13,21},{14,22},{15,23},{16,... | collective-permute-start | bytes 2949128 | tf_op jit(solution)/shard_map/cond/branch_0_fun/ppermute | solution.py:43
  94.7 32.3 %all-to-all-start.2 = ((bf16[8,3,1,48,128]{4,3,2,1,0:T(8,128)(2,1)}), bf16[8,3,1,48,128]{4,3,2,1,0:T(8,128)(2,1)S(1)}, u32[]{:S(2)}, u32[]{:S(2)}) async-start(bf16[8,3,1,48,128]{4,3,2,1,0:T(8,128)(2,1)} %get-tuple-element.40), calls=%async_computation.2 | async-start | bytes 589824 | tf_op jit(solution)/shard_map/cond/branch_0_fun/all_to_all | solution.py:290
  114.5 7.8 %collective-permute-start.6 = (bf16[8,1,2,48,128]{4,3,2,1,0:T(8,128)(2,1)S(1)}, bf16[8,1,2,48,128]{4,3,2,1,0:T(8,128)(2,1)S(1)}, u32[]{:S(2)}, u32[]{:S(2)}) collective-permute-start(bf16[8,1,2,48,128]{4,3,2,1,0:T(8,128)(2,1)S(1)} %get-tuple-element.36), channel_id=1, source_target_pairs={{0,1},{1,0},{2,3},{3,2},{4,5},{5,4},{6,7},{7,6},{8,9},{9,8},{10,11... | collective-permute-start | bytes 589832 | tf_op jit(solution)/shard_map/cond/branch_0_fun/ppermute | solution.py:43
  116.6 8.7 %collective-permute-start.7 = (bf16[8,1,2,48,128]{4,3,2,1,0:T(8,128)(2,1)S(1)}, bf16[8,1,2,48,128]{4,3,2,1,0:T(8,128)(2,1)S(1)}, u32[]{:S(2)}, u32[]{:S(2)}) collective-permute-start(bf16[8,1,2,48,128]{4,3,2,1,0:T(8,128)(2,1)S(1)} %get-tuple-element.37), channel_id=1, source_target_pairs={{1,2},{2,1},{3,4},{4,3},{5,6},{6,5},{9,10},{10,9},{11,12},{12,11},... | collective-permute-start | bytes 589832 | tf_op jit(solution)/shard_map/cond/branch_0_fun/ppermute | solution.py:43
  127.1 19.9 %all-to-all-start.1 = ((bf16[8,3,2,48,128]{4,3,2,1,0:T(8,128)(2,1)}), bf16[8,3,2,48,128]{4,3,2,1,0:T(8,128)(2,1)S(1)}, u32[]{:S(2)}, u32[]{:S(2)}) async-start(bf16[8,3,2,48,128]{4,3,2,1,0:T(8,128)(2,1)} %branch_0_fun.7), calls=%async_computation.1 | async-start | bytes 1179648 | tf_op jit(solution)/shard_map/cond/branch_0_fun/all_to_all | solution.py:290
  148.4 0.7 copy-start.16
where the time goes:
time: 150 us; the launch traced here: 149 us
  waiting for transfers between devices  69.1 us (46%)
  starting transfers between devices  51.6 us (34%)
  Pallas kernels  19.3 us (13%)
  local copies, waits for them, and re-layouts  7.64 us (5%)
    ppermute x8, waiting for transfers between devices, exchange(): return lax.ppermute(value, ('ta', 'ha', 'wa'), pairs)  36.2 us
    all_to_all x4, waiting for transfers between devices, swap(): return lax.all_to_all(blocks, 'ta', split_axis=0, concat_axis=0, tiled=True)  33 us
    all_to_all x4, starting transfers between devices, swap(): return lax.all_to_all(blocks, 'ta', split_axis=0, concat_axis=0, tiled=True)  25.9 us
    ppermute x8, starting transfers between devices, exchange(): return lax.ppermute(value, ('ta', 'ha', 'wa'), pairs)  25.7 us
    pallas_call x1, Pallas kernels, attend(): pl.pallas_call(functools.partial(attend_kernel, full), out_shape=[jax.Sha...  11.8 us
    unnamed x11, local copies, waits for them, and re-layouts  5.32 us
  transfers between devices with their start and end apart: 12, of which 6 were waited for; matrix products, arithmetic and copies ran while one was open for 0% of the time, Pallas kernels for 2%

commit v1 on v0

--- a/solution.py
+++ b/solution.py
@@ -262,7 +262,7 @@
     )(valid, *second, *first)
 
 
-def combine_kernel(valid, own, *refs):
+def combine_kernel(valid, dq, own, *refs):
     first, second, out = refs[0:2], refs[2:4], refs[4]
     full = second[0].shape[1]
     for slot in range(out.shape[1]):
@@ -274,23 +274,31 @@
             for b in range(2):
                 arrived = second[b][:, slot].astype(jnp.float32)
                 total += jnp.where(valid[slot, 3 * b + 3] != 0, arrived, 0.0)
-        out[:, slot] = total.astype(out.dtype)
-
-
-def combine(valid, own, first, second):
+        out[:, slot, 0] = dq[:, slot, 0]
+        out[:, slot, 1:3] = total.astype(out.dtype)
+
+
+def combine(valid, dq, own, first, second):
+    chunks, slots, _, rows, _ = own.shape
     return pl.pallas_call(
         combine_kernel,
-        out_shape=jax.ShapeDtypeStruct(own.shape, own.dtype),
-        in_specs=[smem_spec] + [vmem_spec] * 5,
+        out_shape=jax.ShapeDtypeStruct((chunks, slots, 3, rows, head_dim), own.dtype),
+        in_specs=[smem_spec] + [vmem_spec] * 6,
+        out_specs=vmem_spec,
         compiler_params=small_params,
-    )(valid, own, *first, *second)
+    )(valid, dq, own, *first, *second)
 
 
 def swap(blocks):
     return lax.all_to_all(blocks, "ta", split_axis=0, concat_axis=0, tiled=True)
 
 
-def with_corners(full, order, valid, kv, qg):
+def both_kinds(arrays, which):
+    swapped = {kind: exchange(arrays[kind - 1], which, kind) for kind in (2, 1)}
+    return [swapped[1], swapped[2]]
+
+
+def with_corners(full, valid, kv, qg):
     kv_full = lax.slice_in_dim(kv, 0, full, axis=1)
     second = [exchange(kv_full, 2, kind) for kind in (1, 2)]
     qg, second[0] = lax.optimization_barrier((qg, second[0]))
@@ -298,12 +306,9 @@
     message = jnp.concatenate([kv, *second], axis=1)
     first = [exchange(message, 1, kind) for kind in (1, 2)]
     dq, own, first, second = attend(valid, qg, kv, first, second, full)
-    first = [exchange(first[kind - 1], 1, kind) for kind in (1, 2)]
-    dq = swap(dq)
-    second = relay(valid, second, first)
-    second = [exchange(second[kind - 1], 2, kind) for kind in (1, 2)]
-    dkv = swap(combine(valid, own, first, second))
-    return tuple(unpack(order, dq) + unpack(order, dkv))
+    first = both_kinds(first, 1)
+    second = both_kinds(relay(valid, second, first), 2)
+    return combine(valid, dq, own, first, second)
 
 
 def place_heads(devices, shape, windows, order, valid, choice):
@@ -392,15 +397,18 @@
                 )
 
 
-def prepare_kernel(shape, windows, *refs):
-    sources, (order, valid, choice, kv, qg) = refs[:4], refs[4:]
-    devices, slots = kv.shape[:2]
-    place_heads(devices, shape, windows, order, valid, choice)
+def pack_kernel(order, first, second, packed):
+    devices, slots = packed.shape[:2]
     for rank in range(devices * slots):
         column = pl.multiple_of(order[rank] * head_dim, head_dim)
-        for n, source in enumerate(sources):
-            packed = kv if n < 2 else qg
-            packed[rank % devices, rank // devices, n % 2] = source[:, pl.ds(column, head_dim)]
+        for n, source in enumerate((first, second)):
+            packed[rank % devices, rank // devices, n] = source[:, pl.ds(column, head_dim)]
+
+
+def prepare_kernel(shape, windows, *refs):
+    sources, (order, valid, choice, kv) = refs[:2], refs[2:]
+    place_heads(kv.shape[0], shape, windows, order, valid, choice)
+    pack_kernel(order, *sources, kv)
 
 
 def on_device(query_tokens, key_tokens, value_tokens, grad_output, windows):
@@ -410,23 +418,30 @@
     tokens, features = query_tokens.shape[-2:]
     block = jax.ShapeDtypeStruct((devices, slots, 2, tokens, head_dim), query_tokens.dtype)
     arrays = (key_tokens, value_tokens, query_tokens, grad_output)
+    arrays = [array.reshape(tokens, features) for array in arrays]
     shape = (lax.axis_size("ha"), lax.axis_size("wa"))
-    order, valid, choice, kv, qg = pl.pallas_call(
+    order, valid, choice, kv = pl.pallas_call(
         functools.partial(prepare_kernel, shape),
         out_shape=[
             jax.ShapeDtypeStruct((heads,), jnp.int32),
             jax.ShapeDtypeStruct((slots, 9), jnp.int32),
             jax.ShapeDtypeStruct((1,), jnp.int32),
             block,
-            block,
         ],
-        in_specs=[smem_spec] + [vmem_spec] * 4,
-        out_specs=[smem_spec] * 3 + [vmem_spec] * 2,
+        in_specs=[smem_spec] + [vmem_spec] * 2,
+        out_specs=[smem_spec] * 3 + [vmem_spec],
         compiler_params=small_params,
-    )(windows, *[array.reshape(tokens, features) for array in arrays])
+    )(windows, *arrays[:2])
+    qg = pl.pallas_call(
+        pack_kernel,
+        out_shape=block,
+        in_specs=[smem_spec] + [vmem_spec] * 2,
+        out_specs=vmem_spec,
+        compiler_params=small_params,
+    )(order, *arrays[2:])
     kv = swap(kv)
     branches = [functools.partial(with_corners, full) for full in range(1, slots + 1)]
-    outs = lax.switch(choice[0], branches, order, valid, kv, qg)
+    outs = unpack(order, swap(lax.switch(choice[0], branches, valid, kv, qg)))
     return tuple(out.reshape(query_tokens.shape) for out in outs)
 
 

time: 150 us -> 146 us (0.973)
  the two profiles are of different devices: /device:TPU:89 before, /device:TPU:18 now
where the time goes in v1:
time: 146 us; the launch traced here: 145 us
  waiting for transfers between devices  47.6 us (33%)
  starting transfers between devices  41.5 us (28%)
  blocking collectives  32.5 us (22%)
  Pallas kernels  17.1 us (12%)
  local copies, waits for them, and re-layouts  5.1 us (3%)
    all_to_all x1, blocking collectives, swap(): return lax.all_to_all(blocks, 'ta', split_axis=0, concat_axis=0, tiled=True)  32.5 us
    ppermute x8, waiting for transfers between devices, exchange(): return lax.ppermute(value, ('ta', 'ha', 'wa'), pairs)  30.1 us
    ppermute x8, starting transfers between devices, exchange(): return lax.ppermute(value, ('ta', 'ha', 'wa'), pairs)  27.6 us
    all_to_all x2, waiting for transfers between devices, swap(): return lax.all_to_all(blocks, 'ta', split_axis=0, concat_axis=0, tiled=True)  17.6 us
    all_to_all x2, starting transfers between devices, swap(): return lax.all_to_all(blocks, 'ta', split_axis=0, concat_axis=0, tiled=True)  13.9 us
    pallas_call x1, Pallas kernels, attend(): pl.pallas_call(functools.partial(attend_kernel, full), out_shape=[jax.Sha...  9.8 us
  transfers between devices with their start and end apart: 10, of which 8 were waited for; matrix products, arithmetic and copies ran while one was open for 2% of the time, Pallas kernels for 1%

profile of v1, /device:TPU:18, one launch (start us, length us, event | category | flops | bytes accessed | tf_op | source)
XLA Modules:
  0.0 145.5 jit_solution(6975003659384486238)
XLA Ops:
  0.6 0.8 copy.8.windows
  1.4 1.0 copy-done
  2.4 1.0 copy-done.1
  3.3 2.4 %shard_map.76 = (s32[24]{0:T(128)S(1)}, s32[3,9]{1,0:T(4,128)S(1)}, s32[1]{0:T(128)}, bf16[8,3,2,48,128]{4,3,2,1,0:T(8,128)(2,1)}) custom-call(s32[24,2]{1,0:T(8,128)S(1)} %copy.8.windows, bf16[48,3072]{1,0:T(8,128)(2,1)S(1)} %bitcast.8, bf16[48,3072]{1,0:T(8,128)(2,1)S(1)} %bitcast.9), custom_call_target="tpu_custom_call" | custom-call | tf_op jit(solution)/shard_map/pallas_call | solution.py:423
  5.8 10.3 %all-to-all-start.3 = ((bf16[8,3,2,48,128]{4,3,2,1,0:T(8,128)(2,1)}), bf16[8,3,2,48,128]{4,3,2,1,0:T(8,128)(2,1)S(1)}, u32[]{:S(2)}, u32[]{:S(2)}) async-start(bf16[8,3,2,48,128]{4,3,2,1,0:T(8,128)(2,1)} %get-tuple-element.73), calls=%async_computation.3 | async-start | bytes 1179648 | tf_op jit(solution)/shard_map/all_to_all | solution.py:293
  16.8 1.5 %shard_map.77 = bf16[8,3,2,48,128]{4,3,2,1,0:T(8,128)(2,1)} custom-call(s32[24]{0:T(128)S(1)} %get-tuple-element.71.order, bf16[48,3072]{1,0:T(8,128)(2,1)S(1)} %bitcast.10, bf16[48,3072]{1,0:T(8,128)(2,1)S(1)} %bitcast.11), custom_call_target="tpu_custom_call" | custom-call | tf_op jit(solution)/shard_map/pallas_call | solution.py:435
  18.3 17.6 %all-to-all-done.3 = bf16[8,3,2,48,128]{4,3,2,1,0:T(8,128)(2,1)S(1)} async-done(((bf16[8,3,2,48,128]{4,3,2,1,0:T(8,128)(2,1)}), bf16[8,3,2,48,128]{4,3,2,1,0:T(8,128)(2,1)S(1)}, u32[]{:S(2)}, u32[]{:S(2)}) %all-to-all-start.3) | async-done | bytes 589856 | tf_op jit(solution)/shard_map/all_to_all | solution.py:293
  35.9 75.4 %conditional.1 = (bf16[8,3,3,48,128]{4,3,2,1,0:T(8,128)(2,1)S(1)}) conditional(s32[]{:T(128)} %bitcast.2, (bf16[8,3,2,48,128]{4,3,2,1,0:T(8,128)(2,1)S(1)}, bf16[8,3,2,48,128]{4,3,2,1,0:T(8,128)(2,1)}, s32[3,9]{1,0:T(4,128)S(1)}) %tuple.20, (bf16[8,3,2,48,128]{4,3,2,1,0:T(8,128)(2,1)S(1)}, bf16[8,3,2,48,128]{4,3,2,1,0:T(8,128)(2,1)}, ...), branch_computations={%region_0.0_spmd, %region_1.0_spmd, %region_2.0_spmd} | conditional | flops 5096079360 | bytes 57934180 | solution.py:444
  35.9 2.4 %collective-permute-start = (bf16[8,1,2,48,128]{4,3,2,1,0:T(8,128)(2,1)S(1)}, bf16[8,1,2,48,128]{4,3,2,1,0:T(8,128)(2,1)S(1)}, u32[]{:S(2)}, u32[]{:S(2)}) collective-permute-start(bf16[8,1,2,48,128]{4,3,2,1,0:T(8,128)(2,1)S(1)} %slice.4), channel_id=1, source_target_pairs={{0,1},{1,0},{2,3},{3,2},{4,5},{5,4},{6,7},{7,6},{8,9},{9,8},{10,11... | collective-permute-start | bytes 589832 | tf_op jit(solution)/shard_map/cond/branch_0_fun/ppermute | solution.py:43
  38.3 4.1 %collective-permute-start.1 = (bf16[8,1,2,48,128]{4,3,2,1,0:T(8,128)(2,1)S(1)}, bf16[8,1,2,48,128]{4,3,2,1,0:T(8,128)(2,1)S(1)}, u32[]{:S(2)}, u32[]{:S(2)}) collective-permute-start(bf16[8,1,2,48,128]{4,3,2,1,0:T(8,128)(2,1)S(1)} %slice.4), channel_id=1, source_target_pairs={{1,2},{2,1},{3,4},{4,3},{5,6},{6,5},{9,10},{10,9},{11,12},{12,11},... | collective-permute-start | bytes 589832 | tf_op jit(solution)/shard_map/cond/branch_0_fun/ppermute | solution.py:43
  42.4 1.0 constant_dynamic-update-slice_fusion.2
  43.4 0.1 collective-permute-done.refs_4_
  43.4 3.5 %all-to-all-start = ((bf16[8,3,2,48,128]{4,3,2,1,0:T(8,128)(2,1)}), bf16[8,3,2,48,128]{4,3,2,1,0:T(8,128)(2,1)S(1)}, u32[]{:S(2)}, u32[]{:S(2)}) async-start(bf16[8,3,2,48,128]{4,3,2,1,0:T(8,128)(2,1)} %get-tuple-element.25), calls=%async_computation | async-start | bytes 1179648 | tf_op jit(solution)/shard_map/cond/branch_0_fun/all_to_all | solution.py:293
  47.0 0.7 constant_dynamic-update-slice_fusion.1
  47.7 0.7 constant_dynamic-update-slice_fusion
  48.4 2.3 %collective-permute-start.3 = (bf16[8,5,2,48,128]{4,3,2,1,0:T(8,128)(2,1)}, bf16[8,5,2,48,128]{4,3,2,1,0:T(8,128)(2,1)S(1)}, u32[]{:S(2)}, u32[]{:S(2)}) collective-permute-start(bf16[8,5,2,48,128]{4,3,2,1,0:T(8,128)(2,1)} %constant_dynamic-update-slice_fusion), channel_id=1, source_target_pairs={{8,16},{9,17},{10,18},{11,19},{12,20},{13,21},{14,22},{15,23},{16,... | collective-permute-start | bytes 2949128 | tf_op jit(solution)/shard_map/cond/branch_0_fun/ppermute | solution.py:43
  50.8 5.8 %collective-permute-start.2 = (bf16[8,5,2,48,128]{4,3,2,1,0:T(8,128)(2,1)}, bf16[8,5,2,48,128]{4,3,2,1,0:T(8,128)(2,1)S(1)}, u32[]{:S(2)}, u32[]{:S(2)}) collective-permute-start(bf16[8,5,2,48,128]{4,3,2,1,0:T(8,128)(2,1)} %constant_dynamic-update-slice_fusion), channel_id=1, source_target_pairs={{0,8},{1,9},{2,10},{3,11},{4,12},{5,13},{6,14},{7,15},{8,0},{9,1},... | collective-permute-start | bytes 2949128 | tf_op jit(solution)/shard_map/cond/branch_0_fun/ppermute | solution.py:43
  56.6 8.0 %collective-permute-done.3.refs_3_ = bf16[8,5,2,48,128]{4,3,2,1,0:T(8,128)(2,1)S(1)} collective-permute-done((bf16[8,5,2,48,128]{4,3,2,1,0:T(8,128)(2,1)}, bf16[8,5,2,48,128]{4,3,2,1,0:T(8,128)(2,1)S(1)}, u32[]{:S(2)}, u32[]{:S(2)}) %collective-permute-start.3) | collective-permute-done | bytes 983072 | tf_op jit(solution)/shard_map/cond/branch_0_fun/ppermute | solution.py:43
  64.6 4.3 %collective-permute-done.2.refs_2_ = bf16[8,5,2,48,128]{4,3,2,1,0:T(8,128)(2,1)S(1)} collective-permute-done((bf16[8,5,2,48,128]{4,3,2,1,0:T(8,128)(2,1)}, bf16[8,5,2,48,128]{4,3,2,1,0:T(8,128)(2,1)S(1)}, u32[]{:S(2)}, u32[]{:S(2)}) %collective-permute-start.2) | collective-permute-done | bytes 983072 | tf_op jit(solution)/shard_map/cond/branch_0_fun/ppermute | solution.py:43
  68.9 9.8 %branch_0_fun.3 = (bf16[8,3,1,48,128]{4,3,2,1,0:T(8,128)(2,1)S(1)}, bf16[8,3,2,48,128]{4,3,2,1,0:T(8,128)(2,1)S(1)}, bf16[8,5,2,48,128]{4,3,2,1,0:T(8,128)(2,1)S...) custom-call(s32[3,9]{1,0:T(4,128)S(1)} %get-tuple-element.18.valid, ...), custom_call_target="tpu_custom_call" | custom-call | flops 2831155200 | bytes 8388608 | tf_op jit(solution)/shard_map/cond/branch_0_fun/pallas_call | solution.py:213
  78.7 3.9 %collective-permute-start.4 = (bf16[8,5,2,48,128]{4,3,2,1,0:T(8,128)(2,1)S(1)}, bf16[8,5,2,48,128]{4,3,2,1,0:T(8,128)(2,1)S(1)}, u32[]{:S(2)}, u32[]{:S(2)}) collective-permute-start(bf16[8,5,2,48,128]{4,3,2,1,0:T(8,128)(2,1)S(1)} %get-tuple-element.29), channel_id=1, source_target_pairs={{0,8},{1,9},{2,10},{3,11},{4,12},{5,13},{6,14},{7,15},{8,0},{9,1},... | collective-permute-start | bytes 2949128 | tf_op jit(solution)/shard_map/cond/branch_0_fun/ppermute | solution.py:43
  82.6 1.9 %collective-permute-start.5 = (bf16[8,5,2,48,128]{4,3,2,1,0:T(8,128)(2,1)S(1)}, bf16[8,5,2,48,128]{4,3,2,1,0:T(8,128)(2,1)S(1)}, u32[]{:S(2)}, u32[]{:S(2)}) collective-permute-start(bf16[8,5,2,48,128]{4,3,2,1,0:T(8,128)(2,1)S(1)} %get-tuple-element.30), channel_id=1, source_target_pairs={{8,16},{9,17},{10,18},{11,19},{12,20},{13,21},{14,22},{15,23},{16,... | collective-permute-start | bytes 2949128 | tf_op jit(solution)/shard_map/cond/branch_0_fun/ppermute | solution.py:43
  84.6 10.1 %collective-permute-done.4.refs_2_.refs_0_ = bf16[8,5,2,48,128]{4,3,2,1,0:T(8,128)(2,1)S(1)} collective-permute-done((bf16[8,5,2,48,128]{4,3,2,1,0:T(8,128)(2,1)S(1)}, bf16[8,5,2,48,128]{4,3,2,1,0:T(8,128)(2,1)S(1)}, u32[]{:S(2)}, u32[]{:S(2)}) %collective-permute-start.4) | collective-permute-done | bytes 983072 | tf_op jit(solution)/shard_map/cond/branch_0_fun/ppermute | solution.py:43
  94.7 3.9 %collective-permute-done.5.refs_3_.refs_1_ = bf16[8,5,2,48,128]{4,3,2,1,0:T(8,128)(2,1)S(1)} collective-permute-done((bf16[8,5,2,48,128]{4,3,2,1,0:T(8,128)(2,1)S(1)}, bf16[8,5,2,48,128]{4,3,2,1,0:T(8,128)(2,1)S(1)}, u32[]{:S(2)}, u32[]{:S(2)}) %collective-permute-start.5) | collective-permute-done | bytes 983072 | tf_op jit(solution)/shard_map/cond/branch_0_fun/ppermute | solution.py:43
  98.6 0.8 branch_0_fun.4
  99.4 1.9 %collective-permute-start.6 = (bf16[8,1,2,48,128]{4,3,2,1,0:T(8,128)(2,1)S(1)}, bf16[8,1,2,48,128]{4,3,2,1,0:T(8,128)(2,1)S(1)}, u32[]{:S(2)}, u32[]{:S(2)}) collective-permute-start(bf16[8,1,2,48,128]{4,3,2,1,0:T(8,128)(2,1)S(1)} %get-tuple-element.33), channel_id=1, source_target_pairs={{0,1},{1,0},{2,3},{3,2},{4,5},{5,4},{6,7},{7,6},{8,9},{9,8},{10,11... | collective-permute-start | bytes 589832 | tf_op jit(solution)/shard_map/cond/branch_0_fun/ppermute | solution.py:43
  101.3 5.2 %collective-permute-start.7 = (bf16[8,1,2,48,128]{4,3,2,1,0:T(8,128)(2,1)S(1)}, bf16[8,1,2,48,128]{4,3,2,1,0:T(8,128)(2,1)S(1)}, u32[]{:S(2)}, u32[]{:S(2)}) collective-permute-start(bf16[8,1,2,48,128]{4,3,2,1,0:T(8,128)(2,1)S(1)} %get-tuple-element.34), channel_id=1, source_target_pairs={{1,2},{2,1},{3,4},{4,3},{5,6},{6,5},{9,10},{10,9},{11,12},{12,11},... | collective-permute-start | bytes 589832 | tf_op jit(solution)/shard_map/cond/branch_0_fun/ppermute | solution.py:43
  106.5 0.5 collective-permute-done.6.refs_2_
  107.0 3.2 %collective-permute-done.7.refs_3_ = bf16[8,1,2,48,128]{4,3,2,1,0:T(8,128)(2,1)S(1)} collective-permute-done((bf16[8,1,2,48,128]{4,3,2,1,0:T(8,128)(2,1)S(1)}, bf16[8,1,2,48,128]{4,3,2,1,0:T(8,128)(2,1)S(1)}, u32[]{:S(2)}, u32[]{:S(2)}) %collective-permute-start.7) | collective-permute-done | bytes 196640 | tf_op jit(solution)/shard_map/cond/branch_0_fun/ppermute | solution.py:43
  110.1 0.9 branch_0_fun.5
  111.3 32.5 %all_to_all.24.packed = bf16[8,3,3,48,128]{4,3,2,1,0:T(8,128)(2,1)S(1)} all-to-all(bf16[8,3,3,48,128]{4,3,2,1,0:T(8,128)(2,1)S(1)} %get-tuple-element.78), channel_id=1, replica_groups=mesh['ta'=8,'ha'=8,'wa'=8] {'ta'}, dimensions={0} | all-to-all | bytes 1769472 | tf_op jit(solution)/shard_map/all_to_all | solution.py:293
  143.8 1.7 %shard_map.78 = (bf16[48,3072]{1,0:T(8,128)(2,1)}, bf16[48,3072]{1,0:T(8,128)(2,1)}, bf16[48,3072]{1,0:T(8,128)(2,1)}) custom-call(s32[24]{0:T(128)S(1)} %get-tuple-element.71.order, bf16[8,3,3,48,128]{4,3,2,1,0:T(8,128)(2,1)S(1)} %all_to_all.24.packed), custom_call_target="tpu_custom_call" | custom-call | tf_op jit(solution)/shard_map/pallas_call | solution.py:57
  (9 shorter events, 0.0 us)
Async XLA Ops:
  1.4 1.0 copy-start
  2.4 1.0 copy-start.1
  3.3 13.4 %copy-start.2 = (bf16[1,1,48,3072]{3,2,1,0:T(8,128)(2,1)S(1)}, bf16[1,1,48,3072]{3,2,1,0:T(8,128)(2,1)}, u32[]{:S(2)}) copy-start(bf16[1,1,48,3072]{3,2,1,0:T(8,128)(2,1)} %param.8) | copy-start | bytes 884740
  3.3 13.4 %copy-start.3 = (bf16[1,1,48,3072]{3,2,1,0:T(8,128)(2,1)S(1)}, bf16[1,1,48,3072]{3,2,1,0:T(8,128)(2,1)}, u32[]{:S(2)}) copy-start(bf16[1,1,48,3072]{3,2,1,0:T(8,128)(2,1)} %param.11) | copy-start | bytes 884740
  5.8 30.1 %all-to-all-start.3 = ((bf16[8,3,2,48,128]{4,3,2,1,0:T(8,128)(2,1)}), bf16[8,3,2,48,128]{4,3,2,1,0:T(8,128)(2,1)S(1)}, u32[]{:S(2)}, u32[]{:S(2)}) async-start(bf16[8,3,2,48,128]{4,3,2,1,0:T(8,128)(2,1)} %get-tuple-element.73), calls=%async_computation.3 | async-start | bytes 1179648 | tf_op jit(solution)/shard_map/all_to_all | solution.py:293
  35.9 7.6 %collective-permute-start = (bf16[8,1,2,48,128]{4,3,2,1,0:T(8,128)(2,1)S(1)}, bf16[8,1,2,48,128]{4,3,2,1,0:T(8,128)(2,1)S(1)}, u32[]{:S(2)}, u32[]{:S(2)}) collective-permute-start(bf16[8,1,2,48,128]{4,3,2,1,0:T(8,128)(2,1)S(1)} %slice.4), channel_id=1, source_target_pairs={{0,1},{1,0},{2,3},{3,2},{4,5},{5,4},{6,7},{7,6},{8,9},{9,8},{10,11... | collective-permute-start | bytes 589832 | tf_op jit(solution)/shard_map/cond/branch_0_fun/ppermute | solution.py:43
  38.3 9.4 %collective-permute-start.1 = (bf16[8,1,2,48,128]{4,3,2,1,0:T(8,128)(2,1)S(1)}, bf16[8,1,2,48,128]{4,3,2,1,0:T(8,128)(2,1)S(1)}, u32[]{:S(2)}, u32[]{:S(2)}) collective-permute-start(bf16[8,1,2,48,128]{4,3,2,1,0:T(8,128)(2,1)S(1)} %slice.4), channel_id=1, source_target_pairs={{1,2},{2,1},{3,4},{4,3},{5,6},{6,5},{9,10},{10,9},{11,12},{12,11},... | collective-permute-start | bytes 589832 | tf_op jit(solution)/shard_map/cond/branch_0_fun/ppermute | solution.py:43
  43.4 25.4 %all-to-all-start = ((bf16[8,3,2,48,128]{4,3,2,1,0:T(8,128)(2,1)}), bf16[8,3,2,48,128]{4,3,2,1,0:T(8,128)(2,1)S(1)}, u32[]{:S(2)}, u32[]{:S(2)}) async-start(bf16[8,3,2,48,128]{4,3,2,1,0:T(8,128)(2,1)} %get-tuple-element.25), calls=%async_computation | async-start | bytes 1179648 | tf_op jit(solution)/shard_map/cond/branch_0_fun/all_to_all | solution.py:293
  48.4 16.2 %collective-permute-start.3 = (bf16[8,5,2,48,128]{4,3,2,1,0:T(8,128)(2,1)}, bf16[8,5,2,48,128]{4,3,2,1,0:T(8,128)(2,1)S(1)}, u32[]{:S(2)}, u32[]{:S(2)}) collective-permute-start(bf16[8,5,2,48,128]{4,3,2,1,0:T(8,128)(2,1)} %constant_dynamic-update-slice_fusion), channel_id=1, source_target_pairs={{8,16},{9,17},{10,18},{11,19},{12,20},{13,21},{14,22},{15,23},{16,... | collective-permute-start | bytes 2949128 | tf_op jit(solution)/shard_map/cond/branch_0_fun/ppermute | solution.py:43
  50.8 18.1 %collective-permute-start.2 = (bf16[8,5,2,48,128]{4,3,2,1,0:T(8,128)(2,1)}, bf16[8,5,2,48,128]{4,3,2,1,0:T(8,128)(2,1)S(1)}, u32[]{:S(2)}, u32[]{:S(2)}) collective-permute-start(bf16[8,5,2,48,128]{4,3,2,1,0:T(8,128)(2,1)} %constant_dynamic-update-slice_fusion), channel_id=1, source_target_pairs={{0,8},{1,9},{2,10},{3,11},{4,12},{5,13},{6,14},{7,15},{8,0},{9,1},... | collective-permute-start | bytes 2949128 | tf_op jit(solution)/shard_map/cond/branch_0_fun/ppermute | solution.py:43
  78.7 16.0 %collective-permute-start.4 = (bf16[8,5,2,48,128]{4,3,2,1,0:T(8,128)(2,1)S(1)}, bf16[8,5,2,48,128]{4,3,2,1,0:T(8,128)(2,1)S(1)}, u32[]{:S(2)}, u32[]{:S(2)}) collective-permute-start(bf16[8,5,2,48,128]{4,3,2,1,0:T(8,128)(2,1)S(1)} %get-tuple-element.29), channel_id=1, source_target_pairs={{0,8},{1,9},{2,10},{3,11},{4,12},{5,13},{6,14},{7,15},{8,0},{9,1},... | collective-permute-start | bytes 2949128 | tf_op jit(solution)/shard_map/cond/branch_0_fun/ppermute | solution.py:43
  82.6 16.0 %collective-permute-start.5 = (bf16[8,5,2,48,128]{4,3,2,1,0:T(8,128)(2,1)S(1)}, bf16[8,5,2,48,128]{4,3,2,1,0:T(8,128)(2,1)S(1)}, u32[]{:S(2)}, u32[]{:S(2)}) collective-permute-start(bf16[8,5,2,48,128]{4,3,2,1,0:T(8,128)(2,1)S(1)} %get-tuple-element.30), channel_id=1, source_target_pairs={{8,16},{9,17},{10,18},{11,19},{12,20},{13,21},{14,22},{15,23},{16,... | collective-permute-start | bytes 2949128 | tf_op jit(solution)/shard_map/cond/branch_0_fun/ppermute | solution.py:43
  99.4 7.6 %collective-permute-start.6 = (bf16[8,1,2,48,128]{4,3,2,1,0:T(8,128)(2,1)S(1)}, bf16[8,1,2,48,128]{4,3,2,1,0:T(8,128)(2,1)S(1)}, u32[]{:S(2)}, u32[]{:S(2)}) collective-permute-start(bf16[8,1,2,48,128]{4,3,2,1,0:T(8,128)(2,1)S(1)} %get-tuple-element.33), channel_id=1, source_target_pairs={{0,1},{1,0},{2,3},{3,2},{4,5},{5,4},{6,7},{7,6},{8,9},{9,8},{10,11... | collective-permute-start | bytes 589832 | tf_op jit(solution)/shard_map/cond/branch_0_fun/ppermute | solution.py:43
  101.3 8.8 %collective-permute-start.7 = (bf16[8,1,2,48,128]{4,3,2,1,0:T(8,128)(2,1)S(1)}, bf16[8,1,2,48,128]{4,3,2,1,0:T(8,128)(2,1)S(1)}, u32[]{:S(2)}, u32[]{:S(2)}) collective-permute-start(bf16[8,1,2,48,128]{4,3,2,1,0:T(8,128)(2,1)S(1)} %get-tuple-element.34), channel_id=1, source_target_pairs={{1,2},{2,1},{3,4},{4,3},{5,6},{6,5},{9,10},{10,9},{11,12},{12,11},... | collective-permute-start | bytes 589832 | tf_op jit(solution)/shard_map/cond/branch_0_fun/ppermute | solution.py:43

commit v2 on v1

--- a/solution.py
+++ b/solution.py
@@ -70,28 +70,47 @@
     tile = chunks * rows
     scale = head_dim ** (-0.5)
     to_log2 = scale * log2_e
-    head = pl.ds(0, full)
-    tail = pl.ds(full, slots - full)
-
-    def relayed(b):
-        return pl.ds(slots + b * full, full)
-
-    early = [(qg_in, qg), (own_in, kv.at[0])]
-    early += [(first_in[a].at[:, pl.ds(0, slots)], kv.at[a + 1]) for a in range(2)]
-    late = []
-    for b in range(2):
-        late.append((second_in[b], kv.at[3 * b + 3, :, head]))
-        late += [
-            (first_in[a].at[:, relayed(b)], kv.at[3 * b + 4 + a, :, head]) for a in range(2)
+
+    def pieces(slot, line):
+        here = pl.ds(slot, 1)
+        if line == 0:
+            outside = [(own_in, own_out, here)]
+            outside += [(first_in[a], first_out[a], here) for a in range(2)]
+        else:
+            passed = pl.ds(slots + (line - 1) * full + slot, 1)
+            outside = [(second_in[line - 1], second_out[line - 1], here)]
+            outside += [(first_in[a], first_out[a], passed) for a in range(2)]
+        return [
+            (source.at[:, where], target.at[:, where], 3 * line + a, here)
+            for a, (source, target, where) in enumerate(outside)
         ]
-    early = [pltpu.make_async_copy(*pair, load_sem.at[n]) for n, pair in enumerate(early)]
-    late = [
-        pltpu.make_async_copy(*pair, load_sem.at[len(early) + n]) for n, pair in enumerate(late)
-    ]
-    for copy in early + late:
-        copy.start()
-
-    def over_rows(slot, lines, step):
+
+    def loads(slot, lines):
+        here = pl.ds(slot, 1)
+        copies = [pltpu.make_async_copy(qg_in.at[:, here], qg.at[:, here], load_sem.at[slot, 9])]
+        for line in range(lines):
+            for source, _, place, here in pieces(slot, line):
+                copies.append(
+                    pltpu.make_async_copy(source, kv.at[place, :, here], load_sem.at[slot, place])
+                )
+        return copies
+
+    def stores(slot, line):
+        return [
+            pltpu.make_async_copy(part.at[place, :, here], target, store_sem.at[slot, place])
+            for _, target, place, here in pieces(slot, line)
+        ]
+
+    def dq_store(slot):
+        here = pl.ds(slot, 1)
+        return pltpu.make_async_copy(dq.at[:, here], dq_out.at[:, here], store_sem.at[slot, 9])
+
+    order = [(slot, 1) for slot in range(full, slots)] + [(slot, 3) for slot in range(full)]
+    for slot, lines in order:
+        for copy in loads(slot, lines):
+            copy.start()
+
+    def over_rows(slot, lines, step, after=None):
         def one_line(line, carry):
             start = 3 * line
             here = [valid[slot, start + a] for a in range(3)]
@@ -112,11 +131,15 @@
 
                 lax.fori_loop(0, 3, one_place, 0)
 
+            if after is not None:
+                after(line)
             return carry
 
         lax.fori_loop(0, lines, one_line, 0)
 
     def one_slot(slot, lines):
+        for copy in loads(slot, lines):
+            copy.wait()
         query = qg[:, slot, 0].reshape(tile, head_dim)
         grad = qg[:, slot, 1].reshape(tile, head_dim)
         top[...] = jnp.full(top.shape, -1e30, jnp.float32)
@@ -159,9 +182,18 @@
             part[near, :, slot, 0] = dk.astype(jnp.bfloat16).reshape(shape)
             part[near, :, slot, 1] = dv.astype(jnp.bfloat16).reshape(shape)
 
-        over_rows(slot, lines, backward)
+        def store_line(line):
+            for known in range(lines):
+
+                @pl.when(line == known)
+                def _():
+                    for copy in stores(slot, known):
+                        copy.start()
+
+        over_rows(slot, lines, backward, store_line)
         dq_here = (dq_t[...] * scale).T.astype(jnp.bfloat16)
         dq[:, slot, 0] = dq_here.reshape(chunks, rows, head_dim)
+        dq_store(slot).start()
 
     def tail_slot(slot, carry):
         one_slot(slot, 1)
@@ -171,36 +203,14 @@
         one_slot(slot, 3)
         return carry
 
-    def store(pairs, base):
-        copies = [
-            pltpu.make_async_copy(*pair, store_sem.at[base + n]) for n, pair in enumerate(pairs)
-        ]
-        for copy in copies:
-            copy.start()
-        return copies
-
-    for copy in early:
-        copy.wait()
-    stores = []
     if full < slots:
         lax.fori_loop(full, slots, tail_slot, 0)
-        pairs = [(part.at[0, :, tail], own_out.at[:, tail])]
-        pairs += [(part.at[a + 1, :, tail], first_out[a].at[:, tail]) for a in range(2)]
-        stores += store(pairs, 0)
-    for copy in late:
-        copy.wait()
     lax.fori_loop(0, full, full_slot, 0)
-    pairs = []
-    for a in range(2):
-        pairs.append((part.at[a + 1, :, head], first_out[a].at[:, head]))
-        pairs += [
-            (part.at[3 * b + 4 + a, :, head], first_out[a].at[:, relayed(b)]) for b in range(2)
-        ]
-    pairs += [(part.at[3 * b + 3, :, head], second_out[b]) for b in range(2)]
-    pairs += [(part.at[0, :, head], own_out.at[:, head]), (dq, dq_out)]
-    stores += store(pairs, 3)
-    for copy in stores:
-        copy.wait()
+    for slot, lines in order:
+        for line in range(lines):
+            for copy in stores(slot, line):
+                copy.wait()
+        dq_store(slot).wait()
 
 
 def attend(valid, qg, own, first, second, full):
@@ -227,8 +237,8 @@
             pltpu.VMEM((1, tile), f32),
             pltpu.VMEM((1, tile), f32),
             pltpu.VMEM((head_dim, tile), f32),
-            pltpu.SemaphoreType.DMA((10,)),
-            pltpu.SemaphoreType.DMA((13,)),
+            pltpu.SemaphoreType.DMA((slots, 10)),
+            pltpu.SemaphoreType.DMA((slots, 10)),
         ],
         compiler_params=pltpu.CompilerParams(vmem_limit_bytes=attend_vmem),
         cost_estimate=pl.CostEstimate(

time: 146 us -> 145 us (level)
  the two profiles are of different devices: /device:TPU:18 before, /device:TPU:34 now
where the time goes in v2:
time: 145 us
  waiting for transfers between devices  48.1 us (33%)
  starting transfers between devices  39.2 us (27%)
  blocking collectives  32 us (22%)
  Pallas kernels  18.5 us (13%)
  local copies, waits for them, and re-layouts  5.1 us (4%)
    all_to_all x1, blocking collectives, swap(): return lax.all_to_all(blocks, 'ta', split_axis=0, concat_axis=0, tiled=True)  32 us
    ppermute x8, waiting for transfers between devices, exchange(): return lax.ppermute(value, ('ta', 'ha', 'wa'), pairs)  30.5 us
    ppermute x8, starting transfers between devices, exchange(): return lax.ppermute(value, ('ta', 'ha', 'wa'), pairs)  25.4 us
    all_to_all x2, waiting for transfers between devices, swap(): return lax.all_to_all(blocks, 'ta', split_axis=0, concat_axis=0, tiled=True)  17.6 us
    all_to_all x2, starting transfers between devices, swap(): return lax.all_to_all(blocks, 'ta', split_axis=0, concat_axis=0, tiled=True)  13.9 us
    pallas_call x1, Pallas kernels, attend(): pl.pallas_call(functools.partial(attend_kernel, full), out_shape=[jax.Sha...  11.1 us
  transfers between devices with their start and end apart: 10, of which 8 were waited for; matrix products, arithmetic and copies ran while one was open for 2% of the time, Pallas kernels for 1%

profile of v2, /device:TPU:34, one launch (start us, length us, event | category | flops | bytes accessed | tf_op | source)
XLA Modules:
  0.0 144.5 jit_solution(15777655341539648869)
XLA Ops:
  0.6 0.8 copy.8.windows
  1.4 1.0 copy-done
  2.4 1.0 copy-done.1
  3.3 2.4 %shard_map.76 = (s32[24]{0:T(128)S(1)}, s32[3,9]{1,0:T(4,128)S(1)}, s32[1]{0:T(128)}, bf16[8,3,2,48,128]{4,3,2,1,0:T(8,128)(2,1)}) custom-call(s32[24,2]{1,0:T(8,128)S(1)} %copy.8.windows, bf16[48,3072]{1,0:T(8,128)(2,1)S(1)} %bitcast.8, bf16[48,3072]{1,0:T(8,128)(2,1)S(1)} %bitcast.9), custom_call_target="tpu_custom_call" | custom-call | tf_op jit(solution)/shard_map/pallas_call | solution.py:433
  5.8 10.3 %all-to-all-start.3 = ((bf16[8,3,2,48,128]{4,3,2,1,0:T(8,128)(2,1)}), bf16[8,3,2,48,128]{4,3,2,1,0:T(8,128)(2,1)S(1)}, u32[]{:S(2)}, u32[]{:S(2)}) async-start(bf16[8,3,2,48,128]{4,3,2,1,0:T(8,128)(2,1)} %get-tuple-element.73), calls=%async_computation.3 | async-start | bytes 1179648 | tf_op jit(solution)/shard_map/all_to_all | solution.py:303
  16.8 1.5 %shard_map.77 = bf16[8,3,2,48,128]{4,3,2,1,0:T(8,128)(2,1)} custom-call(s32[24]{0:T(128)S(1)} %get-tuple-element.71.order, bf16[48,3072]{1,0:T(8,128)(2,1)S(1)} %bitcast.10, bf16[48,3072]{1,0:T(8,128)(2,1)S(1)} %bitcast.11), custom_call_target="tpu_custom_call" | custom-call | tf_op jit(solution)/shard_map/pallas_call | solution.py:445
  18.3 17.6 %all-to-all-done.3 = bf16[8,3,2,48,128]{4,3,2,1,0:T(8,128)(2,1)S(1)} async-done(((bf16[8,3,2,48,128]{4,3,2,1,0:T(8,128)(2,1)}), bf16[8,3,2,48,128]{4,3,2,1,0:T(8,128)(2,1)S(1)}, u32[]{:S(2)}, u32[]{:S(2)}) %all-to-all-start.3) | async-done | bytes 589856 | tf_op jit(solution)/shard_map/all_to_all | solution.py:303
  35.9 75.0 %conditional.1 = (bf16[8,3,3,48,128]{4,3,2,1,0:T(8,128)(2,1)S(1)}) conditional(s32[]{:T(128)} %bitcast.2, (bf16[8,3,2,48,128]{4,3,2,1,0:T(8,128)(2,1)S(1)}, bf16[8,3,2,48,128]{4,3,2,1,0:T(8,128)(2,1)}, s32[3,9]{1,0:T(4,128)S(1)}) %tuple.20, (bf16[8,3,2,48,128]{4,3,2,1,0:T(8,128)(2,1)S(1)}, bf16[8,3,2,48,128]{4,3,2,1,0:T(8,128)(2,1)}, ...), branch_computations={%region_0.0_spmd, %region_1.0_spmd, %region_2.0_spmd} | conditional | flops 5096079360 | bytes 57934180 | solution.py:454
  35.9 2.4 %collective-permute-start = (bf16[8,1,2,48,128]{4,3,2,1,0:T(8,128)(2,1)S(1)}, bf16[8,1,2,48,128]{4,3,2,1,0:T(8,128)(2,1)S(1)}, u32[]{:S(2)}, u32[]{:S(2)}) collective-permute-start(bf16[8,1,2,48,128]{4,3,2,1,0:T(8,128)(2,1)S(1)} %slice.4), channel_id=1, source_target_pairs={{0,1},{1,0},{2,3},{3,2},{4,5},{5,4},{6,7},{7,6},{8,9},{9,8},{10,11... | collective-permute-start | bytes 589832 | tf_op jit(solution)/shard_map/cond/branch_0_fun/ppermute | solution.py:43
  38.3 4.1 %collective-permute-start.1 = (bf16[8,1,2,48,128]{4,3,2,1,0:T(8,128)(2,1)S(1)}, bf16[8,1,2,48,128]{4,3,2,1,0:T(8,128)(2,1)S(1)}, u32[]{:S(2)}, u32[]{:S(2)}) collective-permute-start(bf16[8,1,2,48,128]{4,3,2,1,0:T(8,128)(2,1)S(1)} %slice.4), channel_id=1, source_target_pairs={{1,2},{2,1},{3,4},{4,3},{5,6},{6,5},{9,10},{10,9},{11,12},{12,11},... | collective-permute-start | bytes 589832 | tf_op jit(solution)/shard_map/cond/branch_0_fun/ppermute | solution.py:43
  42.4 1.0 constant_dynamic-update-slice_fusion.2
  43.4 0.1 collective-permute-done.refs_4_
  43.4 3.5 %all-to-all-start = ((bf16[8,3,2,48,128]{4,3,2,1,0:T(8,128)(2,1)}), bf16[8,3,2,48,128]{4,3,2,1,0:T(8,128)(2,1)S(1)}, u32[]{:S(2)}, u32[]{:S(2)}) async-start(bf16[8,3,2,48,128]{4,3,2,1,0:T(8,128)(2,1)} %get-tuple-element.25), calls=%async_computation | async-start | bytes 1179648 | tf_op jit(solution)/shard_map/cond/branch_0_fun/all_to_all | solution.py:303
  47.0 0.7 constant_dynamic-update-slice_fusion.1
  47.7 0.7 constant_dynamic-update-slice_fusion
  48.4 2.3 %collective-permute-start.3 = (bf16[8,5,2,48,128]{4,3,2,1,0:T(8,128)(2,1)}, bf16[8,5,2,48,128]{4,3,2,1,0:T(8,128)(2,1)S(1)}, u32[]{:S(2)}, u32[]{:S(2)}) collective-permute-start(bf16[8,5,2,48,128]{4,3,2,1,0:T(8,128)(2,1)} %constant_dynamic-update-slice_fusion), channel_id=1, source_target_pairs={{8,16},{9,17},{10,18},{11,19},{12,20},{13,21},{14,22},{15,23},{16,... | collective-permute-start | bytes 2949128 | tf_op jit(solution)/shard_map/cond/branch_0_fun/ppermute | solution.py:43
  50.8 2.8 %collective-permute-start.2 = (bf16[8,5,2,48,128]{4,3,2,1,0:T(8,128)(2,1)}, bf16[8,5,2,48,128]{4,3,2,1,0:T(8,128)(2,1)S(1)}, u32[]{:S(2)}, u32[]{:S(2)}) collective-permute-start(bf16[8,5,2,48,128]{4,3,2,1,0:T(8,128)(2,1)} %constant_dynamic-update-slice_fusion), channel_id=1, source_target_pairs={{0,8},{1,9},{2,10},{3,11},{4,12},{5,13},{6,14},{7,15},{8,0},{9,1},... | collective-permute-start | bytes 2949128 | tf_op jit(solution)/shard_map/cond/branch_0_fun/ppermute | solution.py:43
  53.6 12.2 %collective-permute-done.3.refs_3_ = bf16[8,5,2,48,128]{4,3,2,1,0:T(8,128)(2,1)S(1)} collective-permute-done((bf16[8,5,2,48,128]{4,3,2,1,0:T(8,128)(2,1)}, bf16[8,5,2,48,128]{4,3,2,1,0:T(8,128)(2,1)S(1)}, u32[]{:S(2)}, u32[]{:S(2)}) %collective-permute-start.3) | collective-permute-done | bytes 983072 | tf_op jit(solution)/shard_map/cond/branch_0_fun/ppermute | solution.py:43
  65.8 1.2 collective-permute-done.2.refs_2_
  67.0 11.1 %branch_0_fun.3 = (bf16[8,3,1,48,128]{4,3,2,1,0:T(8,128)(2,1)S(1)}, bf16[8,3,2,48,128]{4,3,2,1,0:T(8,128)(2,1)S(1)}, bf16[8,5,2,48,128]{4,3,2,1,0:T(8,128)(2,1)S...) custom-call(s32[3,9]{1,0:T(4,128)S(1)} %get-tuple-element.18.valid, ...), custom_call_target="tpu_custom_call" | custom-call | flops 2831155200 | bytes 8388608 | tf_op jit(solution)/shard_map/cond/branch_0_fun/pallas_call | solution.py:223
  78.1 2.8 %collective-permute-start.4 = (bf16[8,5,2,48,128]{4,3,2,1,0:T(8,128)(2,1)S(1)}, bf16[8,5,2,48,128]{4,3,2,1,0:T(8,128)(2,1)S(1)}, u32[]{:S(2)}, u32[]{:S(2)}) collective-permute-start(bf16[8,5,2,48,128]{4,3,2,1,0:T(8,128)(2,1)S(1)} %get-tuple-element.29), channel_id=1, source_target_pairs={{0,8},{1,9},{2,10},{3,11},{4,12},{5,13},{6,14},{7,15},{8,0},{9,1},... | collective-permute-start | bytes 2949128 | tf_op jit(solution)/shard_map/cond/branch_0_fun/ppermute | solution.py:43
  81.0 3.8 %collective-permute-start.5 = (bf16[8,5,2,48,128]{4,3,2,1,0:T(8,128)(2,1)S(1)}, bf16[8,5,2,48,128]{4,3,2,1,0:T(8,128)(2,1)S(1)}, u32[]{:S(2)}, u32[]{:S(2)}) collective-permute-start(bf16[8,5,2,48,128]{4,3,2,1,0:T(8,128)(2,1)S(1)} %get-tuple-element.30), channel_id=1, source_target_pairs={{8,16},{9,17},{10,18},{11,19},{12,20},{13,21},{14,22},{15,23},{16,... | collective-permute-start | bytes 2949128 | tf_op jit(solution)/shard_map/cond/branch_0_fun/ppermute | solution.py:43
  84.8 9.4 %collective-permute-done.4.refs_2_.refs_0_ = bf16[8,5,2,48,128]{4,3,2,1,0:T(8,128)(2,1)S(1)} collective-permute-done((bf16[8,5,2,48,128]{4,3,2,1,0:T(8,128)(2,1)S(1)}, bf16[8,5,2,48,128]{4,3,2,1,0:T(8,128)(2,1)S(1)}, u32[]{:S(2)}, u32[]{:S(2)}) %collective-permute-start.4) | collective-permute-done | bytes 983072 | tf_op jit(solution)/shard_map/cond/branch_0_fun/ppermute | solution.py:43
  94.1 4.0 %collective-permute-done.5.refs_3_.refs_1_ = bf16[8,5,2,48,128]{4,3,2,1,0:T(8,128)(2,1)S(1)} collective-permute-done((bf16[8,5,2,48,128]{4,3,2,1,0:T(8,128)(2,1)S(1)}, bf16[8,5,2,48,128]{4,3,2,1,0:T(8,128)(2,1)S(1)}, u32[]{:S(2)}, u32[]{:S(2)}) %collective-permute-start.5) | collective-permute-done | bytes 983072 | tf_op jit(solution)/shard_map/cond/branch_0_fun/ppermute | solution.py:43
  98.2 0.8 branch_0_fun.4
  98.9 1.9 %collective-permute-start.6 = (bf16[8,1,2,48,128]{4,3,2,1,0:T(8,128)(2,1)S(1)}, bf16[8,1,2,48,128]{4,3,2,1,0:T(8,128)(2,1)S(1)}, u32[]{:S(2)}, u32[]{:S(2)}) collective-permute-start(bf16[8,1,2,48,128]{4,3,2,1,0:T(8,128)(2,1)S(1)} %get-tuple-element.33), channel_id=1, source_target_pairs={{0,1},{1,0},{2,3},{3,2},{4,5},{5,4},{6,7},{7,6},{8,9},{9,8},{10,11... | collective-permute-start | bytes 589832 | tf_op jit(solution)/shard_map/cond/branch_0_fun/ppermute | solution.py:43
  100.9 5.2 %collective-permute-start.7 = (bf16[8,1,2,48,128]{4,3,2,1,0:T(8,128)(2,1)S(1)}, bf16[8,1,2,48,128]{4,3,2,1,0:T(8,128)(2,1)S(1)}, u32[]{:S(2)}, u32[]{:S(2)}) collective-permute-start(bf16[8,1,2,48,128]{4,3,2,1,0:T(8,128)(2,1)S(1)} %get-tuple-element.34), channel_id=1, source_target_pairs={{1,2},{2,1},{3,4},{4,3},{5,6},{6,5},{9,10},{10,9},{11,12},{12,11},... | collective-permute-start | bytes 589832 | tf_op jit(solution)/shard_map/cond/branch_0_fun/ppermute | solution.py:43
  106.0 0.5 collective-permute-done.6.refs_2_
  106.5 3.2 %collective-permute-done.7.refs_3_ = bf16[8,1,2,48,128]{4,3,2,1,0:T(8,128)(2,1)S(1)} collective-permute-done((bf16[8,1,2,48,128]{4,3,2,1,0:T(8,128)(2,1)S(1)}, bf16[8,1,2,48,128]{4,3,2,1,0:T(8,128)(2,1)S(1)}, u32[]{:S(2)}, u32[]{:S(2)}) %collective-permute-start.7) | collective-permute-done | bytes 196640 | tf_op jit(solution)/shard_map/cond/branch_0_fun/ppermute | solution.py:43
  109.7 0.9 branch_0_fun.5
  110.8 32.0 %all_to_all.24.packed = bf16[8,3,3,48,128]{4,3,2,1,0:T(8,128)(2,1)S(1)} all-to-all(bf16[8,3,3,48,128]{4,3,2,1,0:T(8,128)(2,1)S(1)} %get-tuple-element.78), channel_id=1, replica_groups=mesh['ta'=8,'ha'=8,'wa'=8] {'ta'}, dimensions={0} | all-to-all | bytes 1769472 | tf_op jit(solution)/shard_map/all_to_all | solution.py:303
  142.8 1.7 %shard_map.78 = (bf16[48,3072]{1,0:T(8,128)(2,1)}, bf16[48,3072]{1,0:T(8,128)(2,1)}, bf16[48,3072]{1,0:T(8,128)(2,1)}) custom-call(s32[24]{0:T(128)S(1)} %get-tuple-element.71.order, bf16[8,3,3,48,128]{4,3,2,1,0:T(8,128)(2,1)S(1)} %all_to_all.24.packed), custom_call_target="tpu_custom_call" | custom-call | tf_op jit(solution)/shard_map/pallas_call | solution.py:57
  (9 shorter events, 0.0 us)
Async XLA Ops:
  1.4 1.0 copy-start
  2.4 1.0 copy-start.1
  3.3 13.4 %copy-start.2 = (bf16[1,1,48,3072]{3,2,1,0:T(8,128)(2,1)S(1)}, bf16[1,1,48,3072]{3,2,1,0:T(8,128)(2,1)}, u32[]{:S(2)}) copy-start(bf16[1,1,48,3072]{3,2,1,0:T(8,128)(2,1)} %param.8) | copy-start | bytes 884740
  3.3 13.4 %copy-start.3 = (bf16[1,1,48,3072]{3,2,1,0:T(8,128)(2,1)S(1)}, bf16[1,1,48,3072]{3,2,1,0:T(8,128)(2,1)}, u32[]{:S(2)}) copy-start(bf16[1,1,48,3072]{3,2,1,0:T(8,128)(2,1)} %param.11) | copy-start | bytes 884740
  5.8 30.1 %all-to-all-start.3 = ((bf16[8,3,2,48,128]{4,3,2,1,0:T(8,128)(2,1)}), bf16[8,3,2,48,128]{4,3,2,1,0:T(8,128)(2,1)S(1)}, u32[]{:S(2)}, u32[]{:S(2)}) async-start(bf16[8,3,2,48,128]{4,3,2,1,0:T(8,128)(2,1)} %get-tuple-element.73), calls=%async_computation.3 | async-start | bytes 1179648 | tf_op jit(solution)/shard_map/all_to_all | solution.py:303
  35.9 7.6 %collective-permute-start = (bf16[8,1,2,48,128]{4,3,2,1,0:T(8,128)(2,1)S(1)}, bf16[8,1,2,48,128]{4,3,2,1,0:T(8,128)(2,1)S(1)}, u32[]{:S(2)}, u32[]{:S(2)}) collective-permute-start(bf16[8,1,2,48,128]{4,3,2,1,0:T(8,128)(2,1)S(1)} %slice.4), channel_id=1, source_target_pairs={{0,1},{1,0},{2,3},{3,2},{4,5},{5,4},{6,7},{7,6},{8,9},{9,8},{10,11... | collective-permute-start | bytes 589832 | tf_op jit(solution)/shard_map/cond/branch_0_fun/ppermute | solution.py:43
  38.3 9.4 %collective-permute-start.1 = (bf16[8,1,2,48,128]{4,3,2,1,0:T(8,128)(2,1)S(1)}, bf16[8,1,2,48,128]{4,3,2,1,0:T(8,128)(2,1)S(1)}, u32[]{:S(2)}, u32[]{:S(2)}) collective-permute-start(bf16[8,1,2,48,128]{4,3,2,1,0:T(8,128)(2,1)S(1)} %slice.4), channel_id=1, source_target_pairs={{1,2},{2,1},{3,4},{4,3},{5,6},{6,5},{9,10},{10,9},{11,12},{12,11},... | collective-permute-start | bytes 589832 | tf_op jit(solution)/shard_map/cond/branch_0_fun/ppermute | solution.py:43
  43.4 23.5 %all-to-all-start = ((bf16[8,3,2,48,128]{4,3,2,1,0:T(8,128)(2,1)}), bf16[8,3,2,48,128]{4,3,2,1,0:T(8,128)(2,1)S(1)}, u32[]{:S(2)}, u32[]{:S(2)}) async-start(bf16[8,3,2,48,128]{4,3,2,1,0:T(8,128)(2,1)} %get-tuple-element.25), calls=%async_computation | async-start | bytes 1179648 | tf_op jit(solution)/shard_map/cond/branch_0_fun/all_to_all | solution.py:303
  48.4 17.4 %collective-permute-start.3 = (bf16[8,5,2,48,128]{4,3,2,1,0:T(8,128)(2,1)}, bf16[8,5,2,48,128]{4,3,2,1,0:T(8,128)(2,1)S(1)}, u32[]{:S(2)}, u32[]{:S(2)}) collective-permute-start(bf16[8,5,2,48,128]{4,3,2,1,0:T(8,128)(2,1)} %constant_dynamic-update-slice_fusion), channel_id=1, source_target_pairs={{8,16},{9,17},{10,18},{11,19},{12,20},{13,21},{14,22},{15,23},{16,... | collective-permute-start | bytes 2949128 | tf_op jit(solution)/shard_map/cond/branch_0_fun/ppermute | solution.py:43
  50.8 16.2 %collective-permute-start.2 = (bf16[8,5,2,48,128]{4,3,2,1,0:T(8,128)(2,1)}, bf16[8,5,2,48,128]{4,3,2,1,0:T(8,128)(2,1)S(1)}, u32[]{:S(2)}, u32[]{:S(2)}) collective-permute-start(bf16[8,5,2,48,128]{4,3,2,1,0:T(8,128)(2,1)} %constant_dynamic-update-slice_fusion), channel_id=1, source_target_pairs={{0,8},{1,9},{2,10},{3,11},{4,12},{5,13},{6,14},{7,15},{8,0},{9,1},... | collective-permute-start | bytes 2949128 | tf_op jit(solution)/shard_map/cond/branch_0_fun/ppermute | solution.py:43
  78.1 16.0 %collective-permute-start.4 = (bf16[8,5,2,48,128]{4,3,2,1,0:T(8,128)(2,1)S(1)}, bf16[8,5,2,48,128]{4,3,2,1,0:T(8,128)(2,1)S(1)}, u32[]{:S(2)}, u32[]{:S(2)}) collective-permute-start(bf16[8,5,2,48,128]{4,3,2,1,0:T(8,128)(2,1)S(1)} %get-tuple-element.29), channel_id=1, source_target_pairs={{0,8},{1,9},{2,10},{3,11},{4,12},{5,13},{6,14},{7,15},{8,0},{9,1},... | collective-permute-start | bytes 2949128 | tf_op jit(solution)/shard_map/cond/branch_0_fun/ppermute | solution.py:43
  81.0 17.2 %collective-permute-start.5 = (bf16[8,5,2,48,128]{4,3,2,1,0:T(8,128)(2,1)S(1)}, bf16[8,5,2,48,128]{4,3,2,1,0:T(8,128)(2,1)S(1)}, u32[]{:S(2)}, u32[]{:S(2)}) collective-permute-start(bf16[8,5,2,48,128]{4,3,2,1,0:T(8,128)(2,1)S(1)} %get-tuple-element.30), channel_id=1, source_target_pairs={{8,16},{9,17},{10,18},{11,19},{12,20},{13,21},{14,22},{15,23},{16,... | collective-permute-start | bytes 2949128 | tf_op jit(solution)/shard_map/cond/branch_0_fun/ppermute | solution.py:43
  98.9 7.6 %collective-permute-start.6 = (bf16[8,1,2,48,128]{4,3,2,1,0:T(8,128)(2,1)S(1)}, bf16[8,1,2,48,128]{4,3,2,1,0:T(8,128)(2,1)S(1)}, u32[]{:S(2)}, u32[]{:S(2)}) collective-permute-start(bf16[8,1,2,48,128]{4,3,2,1,0:T(8,128)(2,1)S(1)} %get-tuple-element.33), channel_id=1, source_target_pairs={{0,1},{1,0},{2,3},{3,2},{4,5},{5,4},{6,7},{7,6},{8,9},{9,8},{10,11... | collective-permute-start | bytes 589832 | tf_op jit(solution)/shard_map/cond/branch_0_fun/ppermute | solution.py:43
  100.9 8.8 %collective-permute-start.7 = (bf16[8,1,2,48,128]{4,3,2,1,0:T(8,128)(2,1)S(1)}, bf16[8,1,2,48,128]{4,3,2,1,0:T(8,128)(2,1)S(1)}, u32[]{:S(2)}, u32[]{:S(2)}) collective-permute-start(bf16[8,1,2,48,128]{4,3,2,1,0:T(8,128)(2,1)S(1)} %get-tuple-element.34), channel_id=1, source_target_pairs={{1,2},{2,1},{3,4},{4,3},{5,6},{6,5},{9,10},{10,9},{11,12},{12,11},... | collective-permute-start | bytes 589832 | tf_op jit(solution)/shard_map/cond/branch_0_fun/ppermute | solution.py:43

commit v3 on v2

--- a/solution.py
+++ b/solution.py
@@ -65,7 +65,8 @@
 def attend_kernel(full, valid, *refs):
     qg_in, own_in, first_in, second_in = refs[0], refs[1], refs[2:4], refs[4:6]
     dq_out, own_out, first_out, second_out = refs[6], refs[7], refs[8:10], refs[10:12]
-    (qg, kv, score, dprob, part, dq, top, total, weighted, dq_t, load_sem, store_sem) = refs[12:]
+    (qg, kv, score, dprob, part, dq, top, top_then, total, weighted, dq_t) = refs[12:23]
+    load_sem, store_sem = refs[23:]
     chunks, slots, _, rows, _ = qg.shape
     tile = chunks * rows
     scale = head_dim ** (-0.5)
@@ -153,26 +154,27 @@
             value = kv[near, :, slot, 1].reshape(count * tile, head_dim)
             raw = lax.dot_general(key, query, contract_last, preferred_element_type=jnp.float32)
             rise = lax.dot_general(value, grad, contract_last, preferred_element_type=jnp.float32)
-            score[near] = raw.reshape(count, tile, tile)
             dprob[near] = rise.reshape(count, tile, tile)
             top_old = top[...]
             top_new = jnp.maximum(top_old, jnp.max(raw, axis=0, keepdims=True))
             fade = jnp.exp2((top_old - top_new) * to_log2)
             spread = jnp.exp2((raw - top_new) * to_log2)
+            score[near] = spread.reshape(count, tile, tile)
             top[...] = top_new
+            top_then[start] = top_new
             total[...] = total[...] * fade + jnp.sum(spread, axis=0, keepdims=True)
             weighted[...] = weighted[...] * fade + jnp.sum(spread * rise, axis=0, keepdims=True)
 
         over_rows(slot, lines, forward)
-        log_total = top[...] * to_log2 + jnp.log(total[...]) * log2_e
-        delta = weighted[...] / total[...]
+        inverse = 1.0 / total[...]
+        delta = weighted[...] * inverse
 
         def backward(start, count):
             near = pl.ds(start, count)
             key = kv[near, :, slot, 0].reshape(count * tile, head_dim)
-            raw = score[near].reshape(count * tile, tile)
             rise = dprob[near].reshape(count * tile, tile)
-            prob = jnp.exp2(raw * to_log2 - log_total)
+            factor = jnp.exp2((top_then[start] - top[...]) * to_log2) * inverse
+            prob = score[near].reshape(count * tile, tile) * factor
             weight = prob.astype(jnp.bfloat16)
             dscore = (prob * (rise - delta)).astype(jnp.bfloat16)
             dv = jnp.dot(weight, grad, preferred_element_type=jnp.float32)
@@ -234,6 +236,7 @@
             pltpu.VMEM((9,) + own.shape, bf16),
             pltpu.VMEM(dq_shape, bf16),
             pltpu.VMEM((1, tile), f32),
+            pltpu.VMEM((9, 1, tile), f32),
             pltpu.VMEM((1, tile), f32),
             pltpu.VMEM((1, tile), f32),
             pltpu.VMEM((head_dim, tile), f32),
@@ -250,6 +253,25 @@
     return outs[0], outs[1], outs[2:4], outs[4:6]
 
 
+def join_kernel(*refs):
+    out, start = refs[-1], 0
+    for part in refs[:-1]:
+        out[:, start : start + part.shape[1]] = part[...]
+        start += part.shape[1]
+
+
+def join(parts):
+    chunks, _, *rest = parts[0].shape
+    slots = sum(part.shape[1] for part in parts)
+    return pl.pallas_call(
+        join_kernel,
+        out_shape=jax.ShapeDtypeStruct((chunks, slots, *rest), parts[0].dtype),
+        in_specs=[vmem_spec] * len(parts),
+        out_specs=vmem_spec,
+        compiler_params=small_params,
+    )(*parts)
+
+
 def relay_kernel(valid, *refs):
     second, first, out = refs[0:2], refs[2:4], refs[4:6]
     full = out[0].shape[1]
@@ -313,7 +335,7 @@
     second = [exchange(kv_full, 2, kind) for kind in (1, 2)]
     qg, second[0] = lax.optimization_barrier((qg, second[0]))
     qg = swap(qg)
-    message = jnp.concatenate([kv, *second], axis=1)
+    message = join([kv, *second])
     first = [exchange(message, 1, kind) for kind in (1, 2)]
     dq, own, first, second = attend(valid, qg, kv, first, second, full)
     first = both_kinds(first, 1)

time: 145 us -> 146 us (level)
  local copies, waits for them, and re-layouts: 5.1 us -> 2.7 us
  blocking collectives: 32 us -> 34.1 us
  waiting for transfers between devices: 48.1 us -> 49.8 us
    all_to_all x1, blocking collectives: 32 us -> 34.1 us  [swap(): return lax.all_to_all(blocks, 'ta', split_axis=0, concat_axis=0, tiled=True)]
    cond x2 -> x0, local copies, waits for them, and re-layouts: 1.68 us -> none
  transfers between devices with their start and end apart: 10 -> 10, of which waited for: 8 -> 9; matrix products, arithmetic and copies ran while one was open for 2% -> 0% of each run, Pallas kernels for 1% -> 1%
where the time goes in v3:
time: 146 us
  waiting for transfers between devices  49.8 us (34%)
  starting transfers between devices  39 us (27%)
  blocking collectives  34.1 us (23%)
  Pallas kernels  18.6 us (13%)
  local copies, waits for them, and re-layouts  2.7 us (2%)
    all_to_all x1, blocking collectives, swap(): return lax.all_to_all(blocks, 'ta', split_axis=0, concat_axis=0, tiled=True)  34.1 us
    ppermute x8, waiting for transfers between devices, exchange(): return lax.ppermute(value, ('ta', 'ha', 'wa'), pairs)  31.6 us
    ppermute x8, starting transfers between devices, exchange(): return lax.ppermute(value, ('ta', 'ha', 'wa'), pairs)  25.1 us
    all_to_all x2, waiting for transfers between devices, swap(): return lax.all_to_all(blocks, 'ta', split_axis=0, concat_axis=0, tiled=True)  18.2 us
    all_to_all x2, starting transfers between devices, swap(): return lax.all_to_all(blocks, 'ta', split_axis=0, concat_axis=0, tiled=True)  13.9 us
    pallas_call x1, Pallas kernels, attend(): pl.pallas_call(functools.partial(attend_kernel, full), out_shape=[jax.Sha...  11.1 us
  transfers between devices with their start and end apart: 10, of which 9 were waited for; matrix products, arithmetic and copies ran while one was open for 0% of the time, Pallas kernels for 1%

profile of v3, /device:TPU:34, one launch (start us, length us, event | category | flops | bytes accessed | tf_op | source)
XLA Modules:
  0.0 145.8 jit_solution(9773100291260063470)
XLA Ops:
  0.6 0.8 copy.8.windows
  1.4 1.0 copy-done
  2.4 1.0 copy-done.1
  3.3 2.4 %shard_map.76 = (s32[24]{0:T(128)S(1)}, s32[3,9]{1,0:T(4,128)S(1)}, s32[1]{0:T(128)}, bf16[8,3,2,48,128]{4,3,2,1,0:T(8,128)(2,1)}) custom-call(s32[24,2]{1,0:T(8,128)S(1)} %copy.8.windows, bf16[48,3072]{1,0:T(8,128)(2,1)S(1)} %bitcast.8, bf16[48,3072]{1,0:T(8,128)(2,1)S(1)} %bitcast.9), custom_call_target="tpu_custom_call" | custom-call | tf_op jit(solution)/shard_map/pallas_call | solution.py:455
  5.8 10.3 %all-to-all-start.3 = ((bf16[8,3,2,48,128]{4,3,2,1,0:T(8,128)(2,1)}), bf16[8,3,2,48,128]{4,3,2,1,0:T(8,128)(2,1)S(1)}, u32[]{:S(2)}, u32[]{:S(2)}) async-start(bf16[8,3,2,48,128]{4,3,2,1,0:T(8,128)(2,1)} %get-tuple-element.73), calls=%async_computation.3 | async-start | bytes 1179648 | tf_op jit(solution)/shard_map/all_to_all | solution.py:325
  16.8 1.5 %shard_map.77 = bf16[8,3,2,48,128]{4,3,2,1,0:T(8,128)(2,1)} custom-call(s32[24]{0:T(128)S(1)} %get-tuple-element.71.order, bf16[48,3072]{1,0:T(8,128)(2,1)S(1)} %bitcast.10, bf16[48,3072]{1,0:T(8,128)(2,1)S(1)} %bitcast.11), custom_call_target="tpu_custom_call" | custom-call | tf_op jit(solution)/shard_map/pallas_call | solution.py:467
  18.3 17.6 %all-to-all-done.3 = bf16[8,3,2,48,128]{4,3,2,1,0:T(8,128)(2,1)S(1)} async-done(((bf16[8,3,2,48,128]{4,3,2,1,0:T(8,128)(2,1)}), bf16[8,3,2,48,128]{4,3,2,1,0:T(8,128)(2,1)S(1)}, u32[]{:S(2)}, u32[]{:S(2)}) %all-to-all-start.3) | async-done | bytes 589856 | tf_op jit(solution)/shard_map/all_to_all | solution.py:325
  35.9 74.1 %conditional.1 = (bf16[8,3,3,48,128]{4,3,2,1,0:T(8,128)(2,1)S(1)}) conditional(s32[]{:T(128)} %bitcast.2, (bf16[8,3,2,48,128]{4,3,2,1,0:T(8,128)(2,1)S(1)}, bf16[8,3,2,48,128]{4,3,2,1,0:T(8,128)(2,1)}, s32[3,9]{1,0:T(4,128)S(1)}) %tuple.20, (bf16[8,3,2,48,128]{4,3,2,1,0:T(8,128)(2,1)S(1)}, bf16[8,3,2,48,128]{4,3,2,1,0:T(8,128)(2,1)}, ...), branch_computations={%region_0.0_spmd, %region_1.0_spmd, %region_2.0_spmd} | conditional | flops 5096079360 | bytes 54395236 | solution.py:476
  35.9 2.4 %collective-permute-start = (bf16[8,1,2,48,128]{4,3,2,1,0:T(8,128)(2,1)S(1)}, bf16[8,1,2,48,128]{4,3,2,1,0:T(8,128)(2,1)S(1)}, u32[]{:S(2)}, u32[]{:S(2)}) collective-permute-start(bf16[8,1,2,48,128]{4,3,2,1,0:T(8,128)(2,1)S(1)} %slice.4), channel_id=1, source_target_pairs={{0,1},{1,0},{2,3},{3,2},{4,5},{5,4},{6,7},{7,6},{8,9},{9,8},{10,11... | collective-permute-start | bytes 589832 | tf_op jit(solution)/shard_map/cond/branch_0_fun/ppermute | solution.py:43
  38.3 4.1 %collective-permute-start.1 = (bf16[8,1,2,48,128]{4,3,2,1,0:T(8,128)(2,1)S(1)}, bf16[8,1,2,48,128]{4,3,2,1,0:T(8,128)(2,1)S(1)}, u32[]{:S(2)}, u32[]{:S(2)}) collective-permute-start(bf16[8,1,2,48,128]{4,3,2,1,0:T(8,128)(2,1)S(1)} %slice.4), channel_id=1, source_target_pairs={{1,2},{2,1},{3,4},{4,3},{5,6},{6,5},{9,10},{10,9},{11,12},{12,11},... | collective-permute-start | bytes 589832 | tf_op jit(solution)/shard_map/cond/branch_0_fun/ppermute | solution.py:43
  42.4 1.0 collective-permute-done.refs_1_.refs_4_
  43.4 3.5 %all-to-all-start = ((bf16[8,3,2,48,128]{4,3,2,1,0:T(8,128)(2,1)}), bf16[8,3,2,48,128]{4,3,2,1,0:T(8,128)(2,1)S(1)}, u32[]{:S(2)}, u32[]{:S(2)}) async-start(bf16[8,3,2,48,128]{4,3,2,1,0:T(8,128)(2,1)} %get-tuple-element.25), calls=%async_computation | async-start | bytes 1179648 | tf_op jit(solution)/shard_map/cond/branch_0_fun/all_to_all | solution.py:325
  47.0 0.0 collective-permute-done.1.refs_2_.refs_5_
  47.0 0.1 branch_0_fun.4
  47.1 2.4 %collective-permute-start.3 = (bf16[8,5,2,48,128]{4,3,2,1,0:T(8,128)(2,1)S(1)}, bf16[8,5,2,48,128]{4,3,2,1,0:T(8,128)(2,1)S(1)}, u32[]{:S(2)}, u32[]{:S(2)}) collective-permute-start(bf16[8,5,2,48,128]{4,3,2,1,0:T(8,128)(2,1)S(1)} %branch_0_fun.4), channel_id=1, source_target_pairs={{8,16},{9,17},{10,18},{11,19},{12,20},{13,21},{14,22},{15,23},{16,... | collective-permute-start | bytes 2949128 | tf_op jit(solution)/shard_map/cond/branch_0_fun/ppermute | solution.py:43
  49.4 2.8 %collective-permute-start.2 = (bf16[8,5,2,48,128]{4,3,2,1,0:T(8,128)(2,1)S(1)}, bf16[8,5,2,48,128]{4,3,2,1,0:T(8,128)(2,1)S(1)}, u32[]{:S(2)}, u32[]{:S(2)}) collective-permute-start(bf16[8,5,2,48,128]{4,3,2,1,0:T(8,128)(2,1)S(1)} %branch_0_fun.4), channel_id=1, source_target_pairs={{0,8},{1,9},{2,10},{3,11},{4,12},{5,13},{6,14},{7,15},{8,0},{9,1},... | collective-permute-start | bytes 2949128 | tf_op jit(solution)/shard_map/cond/branch_0_fun/ppermute | solution.py:43
  52.3 12.0 %collective-permute-done.3.refs_3_ = bf16[8,5,2,48,128]{4,3,2,1,0:T(8,128)(2,1)S(1)} collective-permute-done((bf16[8,5,2,48,128]{4,3,2,1,0:T(8,128)(2,1)S(1)}, bf16[8,5,2,48,128]{4,3,2,1,0:T(8,128)(2,1)S(1)}, u32[]{:S(2)}, u32[]{:S(2)}) %collective-permute-start.3) | collective-permute-done | bytes 983072 | tf_op jit(solution)/shard_map/cond/branch_0_fun/ppermute | solution.py:43
  64.3 1.2 collective-permute-done.2.refs_2_
  65.4 0.6 all-to-all-done.refs_0_
  66.0 11.1 %branch_0_fun.5 = (bf16[8,3,1,48,128]{4,3,2,1,0:T(8,128)(2,1)S(1)}, bf16[8,3,2,48,128]{4,3,2,1,0:T(8,128)(2,1)S(1)}, bf16[8,5,2,48,128]{4,3,2,1,0:T(8,128)(2,1)S...) custom-call(s32[3,9]{1,0:T(4,128)S(1)} %get-tuple-element.18.valid, ...), custom_call_target="tpu_custom_call" | custom-call | flops 2831155200 | bytes 8388608 | tf_op jit(solution)/shard_map/cond/branch_0_fun/pallas_call | solution.py:225
  77.2 2.6 %collective-permute-start.4 = (bf16[8,5,2,48,128]{4,3,2,1,0:T(8,128)(2,1)S(1)}, bf16[8,5,2,48,128]{4,3,2,1,0:T(8,128)(2,1)S(1)}, u32[]{:S(2)}, u32[]{:S(2)}) collective-permute-start(bf16[8,5,2,48,128]{4,3,2,1,0:T(8,128)(2,1)S(1)} %get-tuple-element.29), channel_id=1, source_target_pairs={{0,8},{1,9},{2,10},{3,11},{4,12},{5,13},{6,14},{7,15},{8,0},{9,1},... | collective-permute-start | bytes 2949128 | tf_op jit(solution)/shard_map/cond/branch_0_fun/ppermute | solution.py:43
  79.8 3.4 %collective-permute-start.5 = (bf16[8,5,2,48,128]{4,3,2,1,0:T(8,128)(2,1)S(1)}, bf16[8,5,2,48,128]{4,3,2,1,0:T(8,128)(2,1)S(1)}, u32[]{:S(2)}, u32[]{:S(2)}) collective-permute-start(bf16[8,5,2,48,128]{4,3,2,1,0:T(8,128)(2,1)S(1)} %get-tuple-element.30), channel_id=1, source_target_pairs={{8,16},{9,17},{10,18},{11,19},{12,20},{13,21},{14,22},{15,23},{16,... | collective-permute-start | bytes 2949128 | tf_op jit(solution)/shard_map/cond/branch_0_fun/ppermute | solution.py:43
  83.2 9.9 %collective-permute-done.4.refs_2_.refs_0_ = bf16[8,5,2,48,128]{4,3,2,1,0:T(8,128)(2,1)S(1)} collective-permute-done((bf16[8,5,2,48,128]{4,3,2,1,0:T(8,128)(2,1)S(1)}, bf16[8,5,2,48,128]{4,3,2,1,0:T(8,128)(2,1)S(1)}, u32[]{:S(2)}, u32[]{:S(2)}) %collective-permute-start.4) | collective-permute-done | bytes 983072 | tf_op jit(solution)/shard_map/cond/branch_0_fun/ppermute | solution.py:43
  93.2 3.8 %collective-permute-done.5.refs_3_.refs_1_ = bf16[8,5,2,48,128]{4,3,2,1,0:T(8,128)(2,1)S(1)} collective-permute-done((bf16[8,5,2,48,128]{4,3,2,1,0:T(8,128)(2,1)S(1)}, bf16[8,5,2,48,128]{4,3,2,1,0:T(8,128)(2,1)S(1)}, u32[]{:S(2)}, u32[]{:S(2)}) %collective-permute-start.5) | collective-permute-done | bytes 983072 | tf_op jit(solution)/shard_map/cond/branch_0_fun/ppermute | solution.py:43
  97.0 0.8 branch_0_fun.6
  97.8 1.9 %collective-permute-start.6 = (bf16[8,1,2,48,128]{4,3,2,1,0:T(8,128)(2,1)S(1)}, bf16[8,1,2,48,128]{4,3,2,1,0:T(8,128)(2,1)S(1)}, u32[]{:S(2)}, u32[]{:S(2)}) collective-permute-start(bf16[8,1,2,48,128]{4,3,2,1,0:T(8,128)(2,1)S(1)} %get-tuple-element.33), channel_id=1, source_target_pairs={{0,1},{1,0},{2,3},{3,2},{4,5},{5,4},{6,7},{7,6},{8,9},{9,8},{10,11... | collective-permute-start | bytes 589832 | tf_op jit(solution)/shard_map/cond/branch_0_fun/ppermute | solution.py:43
  99.7 5.5 %collective-permute-start.7 = (bf16[8,1,2,48,128]{4,3,2,1,0:T(8,128)(2,1)S(1)}, bf16[8,1,2,48,128]{4,3,2,1,0:T(8,128)(2,1)S(1)}, u32[]{:S(2)}, u32[]{:S(2)}) collective-permute-start(bf16[8,1,2,48,128]{4,3,2,1,0:T(8,128)(2,1)S(1)} %get-tuple-element.34), channel_id=1, source_target_pairs={{1,2},{2,1},{3,4},{4,3},{5,6},{6,5},{9,10},{10,9},{11,12},{12,11},... | collective-permute-start | bytes 589832 | tf_op jit(solution)/shard_map/cond/branch_0_fun/ppermute | solution.py:43
  105.2 0.1 collective-permute-done.6.refs_2_
  105.3 3.5 %collective-permute-done.7.refs_3_ = bf16[8,1,2,48,128]{4,3,2,1,0:T(8,128)(2,1)S(1)} collective-permute-done((bf16[8,1,2,48,128]{4,3,2,1,0:T(8,128)(2,1)S(1)}, bf16[8,1,2,48,128]{4,3,2,1,0:T(8,128)(2,1)S(1)}, u32[]{:S(2)}, u32[]{:S(2)}) %collective-permute-start.7) | collective-permute-done | bytes 196640 | tf_op jit(solution)/shard_map/cond/branch_0_fun/ppermute | solution.py:43
  108.8 0.9 branch_0_fun.7
  110.0 34.1 %all_to_all.24.packed = bf16[8,3,3,48,128]{4,3,2,1,0:T(8,128)(2,1)S(1)} all-to-all(bf16[8,3,3,48,128]{4,3,2,1,0:T(8,128)(2,1)S(1)} %get-tuple-element.78), channel_id=1, replica_groups=mesh['ta'=8,'ha'=8,'wa'=8] {'ta'}, dimensions={0} | all-to-all | bytes 1769472 | tf_op jit(solution)/shard_map/all_to_all | solution.py:325
  144.1 1.7 %shard_map.78 = (bf16[48,3072]{1,0:T(8,128)(2,1)}, bf16[48,3072]{1,0:T(8,128)(2,1)}, bf16[48,3072]{1,0:T(8,128)(2,1)}) custom-call(s32[24]{0:T(128)S(1)} %get-tuple-element.71.order, bf16[8,3,3,48,128]{4,3,2,1,0:T(8,128)(2,1)S(1)} %all_to_all.24.packed), custom_call_target="tpu_custom_call" | custom-call | tf_op jit(solution)/shard_map/pallas_call | solution.py:57
  (7 shorter events, 0.0 us)
Async XLA Ops:
  1.4 1.0 copy-start
  2.4 1.0 copy-start.1
  3.3 13.4 %copy-start.2 = (bf16[1,1,48,3072]{3,2,1,0:T(8,128)(2,1)S(1)}, bf16[1,1,48,3072]{3,2,1,0:T(8,128)(2,1)}, u32[]{:S(2)}) copy-start(bf16[1,1,48,3072]{3,2,1,0:T(8,128)(2,1)} %param.8) | copy-start | bytes 884740
  3.3 13.4 %copy-start.3 = (bf16[1,1,48,3072]{3,2,1,0:T(8,128)(2,1)S(1)}, bf16[1,1,48,3072]{3,2,1,0:T(8,128)(2,1)}, u32[]{:S(2)}) copy-start(bf16[1,1,48,3072]{3,2,1,0:T(8,128)(2,1)} %param.11) | copy-start | bytes 884740
  5.8 30.1 %all-to-all-start.3 = ((bf16[8,3,2,48,128]{4,3,2,1,0:T(8,128)(2,1)}), bf16[8,3,2,48,128]{4,3,2,1,0:T(8,128)(2,1)S(1)}, u32[]{:S(2)}, u32[]{:S(2)}) async-start(bf16[8,3,2,48,128]{4,3,2,1,0:T(8,128)(2,1)} %get-tuple-element.73), calls=%async_computation.3 | async-start | bytes 1179648 | tf_op jit(solution)/shard_map/all_to_all | solution.py:325
  35.9 7.6 %collective-permute-start = (bf16[8,1,2,48,128]{4,3,2,1,0:T(8,128)(2,1)S(1)}, bf16[8,1,2,48,128]{4,3,2,1,0:T(8,128)(2,1)S(1)}, u32[]{:S(2)}, u32[]{:S(2)}) collective-permute-start(bf16[8,1,2,48,128]{4,3,2,1,0:T(8,128)(2,1)S(1)} %slice.4), channel_id=1, source_target_pairs={{0,1},{1,0},{2,3},{3,2},{4,5},{5,4},{6,7},{7,6},{8,9},{9,8},{10,11... | collective-permute-start | bytes 589832 | tf_op jit(solution)/shard_map/cond/branch_0_fun/ppermute | solution.py:43
  38.3 8.7 %collective-permute-start.1 = (bf16[8,1,2,48,128]{4,3,2,1,0:T(8,128)(2,1)S(1)}, bf16[8,1,2,48,128]{4,3,2,1,0:T(8,128)(2,1)S(1)}, u32[]{:S(2)}, u32[]{:S(2)}) collective-permute-start(bf16[8,1,2,48,128]{4,3,2,1,0:T(8,128)(2,1)S(1)} %slice.4), channel_id=1, source_target_pairs={{1,2},{2,1},{3,4},{4,3},{5,6},{6,5},{9,10},{10,9},{11,12},{12,11},... | collective-permute-start | bytes 589832 | tf_op jit(solution)/shard_map/cond/branch_0_fun/ppermute | solution.py:43
  43.4 22.6 %all-to-all-start = ((bf16[8,3,2,48,128]{4,3,2,1,0:T(8,128)(2,1)}), bf16[8,3,2,48,128]{4,3,2,1,0:T(8,128)(2,1)S(1)}, u32[]{:S(2)}, u32[]{:S(2)}) async-start(bf16[8,3,2,48,128]{4,3,2,1,0:T(8,128)(2,1)} %get-tuple-element.25), calls=%async_computation | async-start | bytes 1179648 | tf_op jit(solution)/shard_map/cond/branch_0_fun/all_to_all | solution.py:325
  47.1 17.2 %collective-permute-start.3 = (bf16[8,5,2,48,128]{4,3,2,1,0:T(8,128)(2,1)S(1)}, bf16[8,5,2,48,128]{4,3,2,1,0:T(8,128)(2,1)S(1)}, u32[]{:S(2)}, u32[]{:S(2)}) collective-permute-start(bf16[8,5,2,48,128]{4,3,2,1,0:T(8,128)(2,1)S(1)} %branch_0_fun.4), channel_id=1, source_target_pairs={{8,16},{9,17},{10,18},{11,19},{12,20},{13,21},{14,22},{15,23},{16,... | collective-permute-start | bytes 2949128 | tf_op jit(solution)/shard_map/cond/branch_0_fun/ppermute | solution.py:43
  49.4 16.0 %collective-permute-start.2 = (bf16[8,5,2,48,128]{4,3,2,1,0:T(8,128)(2,1)S(1)}, bf16[8,5,2,48,128]{4,3,2,1,0:T(8,128)(2,1)S(1)}, u32[]{:S(2)}, u32[]{:S(2)}) collective-permute-start(bf16[8,5,2,48,128]{4,3,2,1,0:T(8,128)(2,1)S(1)} %branch_0_fun.4), channel_id=1, source_target_pairs={{0,8},{1,9},{2,10},{3,11},{4,12},{5,13},{6,14},{7,15},{8,0},{9,1},... | collective-permute-start | bytes 2949128 | tf_op jit(solution)/shard_map/cond/branch_0_fun/ppermute | solution.py:43
  77.2 16.0 %collective-permute-start.4 = (bf16[8,5,2,48,128]{4,3,2,1,0:T(8,128)(2,1)S(1)}, bf16[8,5,2,48,128]{4,3,2,1,0:T(8,128)(2,1)S(1)}, u32[]{:S(2)}, u32[]{:S(2)}) collective-permute-start(bf16[8,5,2,48,128]{4,3,2,1,0:T(8,128)(2,1)S(1)} %get-tuple-element.29), channel_id=1, source_target_pairs={{0,8},{1,9},{2,10},{3,11},{4,12},{5,13},{6,14},{7,15},{8,0},{9,1},... | collective-permute-start | bytes 2949128 | tf_op jit(solution)/shard_map/cond/branch_0_fun/ppermute | solution.py:43
  79.8 17.2 %collective-permute-start.5 = (bf16[8,5,2,48,128]{4,3,2,1,0:T(8,128)(2,1)S(1)}, bf16[8,5,2,48,128]{4,3,2,1,0:T(8,128)(2,1)S(1)}, u32[]{:S(2)}, u32[]{:S(2)}) collective-permute-start(bf16[8,5,2,48,128]{4,3,2,1,0:T(8,128)(2,1)S(1)} %get-tuple-element.30), channel_id=1, source_target_pairs={{8,16},{9,17},{10,18},{11,19},{12,20},{13,21},{14,22},{15,23},{16,... | collective-permute-start | bytes 2949128 | tf_op jit(solution)/shard_map/cond/branch_0_fun/ppermute | solution.py:43
  97.8 7.6 %collective-permute-start.6 = (bf16[8,1,2,48,128]{4,3,2,1,0:T(8,128)(2,1)S(1)}, bf16[8,1,2,48,128]{4,3,2,1,0:T(8,128)(2,1)S(1)}, u32[]{:S(2)}, u32[]{:S(2)}) collective-permute-start(bf16[8,1,2,48,128]{4,3,2,1,0:T(8,128)(2,1)S(1)} %get-tuple-element.33), channel_id=1, source_target_pairs={{0,1},{1,0},{2,3},{3,2},{4,5},{5,4},{6,7},{7,6},{8,9},{9,8},{10,11... | collective-permute-start | bytes 589832 | tf_op jit(solution)/shard_map/cond/branch_0_fun/ppermute | solution.py:43
  99.7 9.1 %collective-permute-start.7 = (bf16[8,1,2,48,128]{4,3,2,1,0:T(8,128)(2,1)S(1)}, bf16[8,1,2,48,128]{4,3,2,1,0:T(8,128)(2,1)S(1)}, u32[]{:S(2)}, u32[]{:S(2)}) collective-permute-start(bf16[8,1,2,48,128]{4,3,2,1,0:T(8,128)(2,1)S(1)} %get-tuple-element.34), channel_id=1, source_target_pairs={{1,2},{2,1},{3,4},{4,3},{5,6},{6,5},{9,10},{10,9},{11,12},{12,11},... | collective-permute-start | bytes 589832 | tf_op jit(solution)/shard_map/cond/branch_0_fun/ppermute | solution.py:43

commit v4 on v3

--- a/solution.py
+++ b/solution.py
@@ -13,6 +13,7 @@
 contract_last = (((1,), (1,)), ((), ()))
 small_vmem = 12 * 1024 * 1024
 attend_vmem = 44 * 1024 * 1024
+whole_vmem = 60 * 1024 * 1024
 hbm_spec = pl.BlockSpec(memory_space=pltpu.HBM)
 vmem_spec = pl.BlockSpec(memory_space=pltpu.VMEM)
 smem_spec = pl.BlockSpec(memory_space=pltpu.SMEM)
@@ -462,7 +463,7 @@
         ],
         in_specs=[smem_spec] + [vmem_spec] * 2,
         out_specs=[smem_spec] * 3 + [vmem_spec],
-        compiler_params=small_params,
+        compiler_params=pltpu.CompilerParams(vmem_limit_bytes=whole_vmem),
     )(windows, *arrays[:2])
     qg = pl.pallas_call(
         pack_kernel,

time: 146 us -> 145 us (level)
  no operation moved by 1% of the time
where the time goes in v4:
time: 145 us
  waiting for transfers between devices  49.1 us (34%)
  starting transfers between devices  39 us (27%)
  blocking collectives  34.1 us (24%)
  Pallas kernels  18.9 us (13%)
  local copies, waits for them, and re-layouts  2.09 us (1%)
    all_to_all x1, blocking collectives, swap(): return lax.all_to_all(blocks, 'ta', split_axis=0, concat_axis=0, tiled=True)  34.1 us
    ppermute x8, waiting for transfers between devices, exchange(): return lax.ppermute(value, ('ta', 'ha', 'wa'), pairs)  31.6 us
    ppermute x8, starting transfers between devices, exchange(): return lax.ppermute(value, ('ta', 'ha', 'wa'), pairs)  25.1 us
    all_to_all x2, waiting for transfers between devices, swap(): return lax.all_to_all(blocks, 'ta', split_axis=0, concat_axis=0, tiled=True)  17.5 us
    all_to_all x2, starting transfers between devices, swap(): return lax.all_to_all(blocks, 'ta', split_axis=0, concat_axis=0, tiled=True)  13.9 us
    pallas_call x1, Pallas kernels, attend(): pl.pallas_call(functools.partial(attend_kernel, full), out_shape=[jax.Sha...  11.2 us
  transfers between devices with their start and end apart: 10, of which 9 were waited for; matrix products, arithmetic and copies ran while one was open for 0% of the time, Pallas kernels for 1%

profile of v4, /device:TPU:34, one launch (start us, length us, event | category | flops | bytes accessed | tf_op | source)
XLA Modules:
  0.0 144.9 jit_solution(188308772729528820)
XLA Ops:
  0.7 1.4 copy.8.windows
  2.1 2.8 %shard_map.76 = (s32[24]{0:T(128)}, s32[3,9]{1,0:T(4,128)S(1)}, s32[1]{0:T(128)}, bf16[8,3,2,48,128]{4,3,2,1,0:T(8,128)(2,1)}) custom-call(s32[24,2]{1,0:T(8,128)} %copy.8.windows, bf16[48,3072]{1,0:T(8,128)(2,1)} %bitcast.10, bf16[48,3072]{1,0:T(8,128)(2,1)} %bitcast.11), custom_call_target="tpu_custom_call" | custom-call | tf_op jit(solution)/shard_map/pallas_call | solution.py:456
  4.8 10.3 %all-to-all-start.3 = ((bf16[8,3,2,48,128]{4,3,2,1,0:T(8,128)(2,1)}), bf16[8,3,2,48,128]{4,3,2,1,0:T(8,128)(2,1)S(1)}, u32[]{:S(2)}, u32[]{:S(2)}) async-start(bf16[8,3,2,48,128]{4,3,2,1,0:T(8,128)(2,1)} %get-tuple-element.73), calls=%async_computation.3 | async-start | bytes 1179648 | tf_op jit(solution)/shard_map/all_to_all | solution.py:326
  15.8 0.0 copy-start.2
  15.8 0.6 copy-done.2
  16.5 1.5 %shard_map.77 = bf16[8,3,2,48,128]{4,3,2,1,0:T(8,128)(2,1)} custom-call(s32[24]{0:T(128)S(1)} %copy-done.2, bf16[48,3072]{1,0:T(8,128)(2,1)S(1)} %bitcast.8, bf16[48,3072]{1,0:T(8,128)(2,1)S(1)} %bitcast.9), custom_call_target="tpu_custom_call" | custom-call | tf_op jit(solution)/shard_map/pallas_call | solution.py:468
  18.0 16.9 %all-to-all-done.3 = bf16[8,3,2,48,128]{4,3,2,1,0:T(8,128)(2,1)S(1)} async-done(((bf16[8,3,2,48,128]{4,3,2,1,0:T(8,128)(2,1)}), bf16[8,3,2,48,128]{4,3,2,1,0:T(8,128)(2,1)S(1)}, u32[]{:S(2)}, u32[]{:S(2)}) %all-to-all-start.3) | async-done | bytes 589856 | tf_op jit(solution)/shard_map/all_to_all | solution.py:326
  34.9 74.1 %conditional.1 = (bf16[8,3,3,48,128]{4,3,2,1,0:T(8,128)(2,1)S(1)}) conditional(s32[]{:T(128)} %bitcast.2, (bf16[8,3,2,48,128]{4,3,2,1,0:T(8,128)(2,1)S(1)}, bf16[8,3,2,48,128]{4,3,2,1,0:T(8,128)(2,1)}, s32[3,9]{1,0:T(4,128)S(1)}) %tuple.20, (bf16[8,3,2,48,128]{4,3,2,1,0:T(8,128)(2,1)S(1)}, bf16[8,3,2,48,128]{4,3,2,1,0:T(8,128)(2,1)}, ...), branch_computations={%region_0.0_spmd, %region_1.0_spmd, %region_2.0_spmd} | conditional | flops 5096079360 | bytes 54395236 | solution.py:477
  35.0 2.4 %collective-permute-start = (bf16[8,1,2,48,128]{4,3,2,1,0:T(8,128)(2,1)S(1)}, bf16[8,1,2,48,128]{4,3,2,1,0:T(8,128)(2,1)S(1)}, u32[]{:S(2)}, u32[]{:S(2)}) collective-permute-start(bf16[8,1,2,48,128]{4,3,2,1,0:T(8,128)(2,1)S(1)} %slice.4), channel_id=1, source_target_pairs={{0,1},{1,0},{2,3},{3,2},{4,5},{5,4},{6,7},{7,6},{8,9},{9,8},{10,11... | collective-permute-start | bytes 589832 | tf_op jit(solution)/shard_map/cond/branch_0_fun/ppermute | solution.py:44
  37.4 4.1 %collective-permute-start.1 = (bf16[8,1,2,48,128]{4,3,2,1,0:T(8,128)(2,1)S(1)}, bf16[8,1,2,48,128]{4,3,2,1,0:T(8,128)(2,1)S(1)}, u32[]{:S(2)}, u32[]{:S(2)}) collective-permute-start(bf16[8,1,2,48,128]{4,3,2,1,0:T(8,128)(2,1)S(1)} %slice.4), channel_id=1, source_target_pairs={{1,2},{2,1},{3,4},{4,3},{5,6},{6,5},{9,10},{10,9},{11,12},{12,11},... | collective-permute-start | bytes 589832 | tf_op jit(solution)/shard_map/cond/branch_0_fun/ppermute | solution.py:44
  41.5 1.0 collective-permute-done.refs_1_.refs_4_
  42.5 3.5 %all-to-all-start = ((bf16[8,3,2,48,128]{4,3,2,1,0:T(8,128)(2,1)}), bf16[8,3,2,48,128]{4,3,2,1,0:T(8,128)(2,1)S(1)}, u32[]{:S(2)}, u32[]{:S(2)}) async-start(bf16[8,3,2,48,128]{4,3,2,1,0:T(8,128)(2,1)} %get-tuple-element.25), calls=%async_computation | async-start | bytes 1179648 | tf_op jit(solution)/shard_map/cond/branch_0_fun/all_to_all | solution.py:326
  46.1 0.1 branch_0_fun.4
  46.1 2.4 %collective-permute-start.3 = (bf16[8,5,2,48,128]{4,3,2,1,0:T(8,128)(2,1)S(1)}, bf16[8,5,2,48,128]{4,3,2,1,0:T(8,128)(2,1)S(1)}, u32[]{:S(2)}, u32[]{:S(2)}) collective-permute-start(bf16[8,5,2,48,128]{4,3,2,1,0:T(8,128)(2,1)S(1)} %branch_0_fun.4), channel_id=1, source_target_pairs={{8,16},{9,17},{10,18},{11,19},{12,20},{13,21},{14,22},{15,23},{16,... | collective-permute-start | bytes 2949128 | tf_op jit(solution)/shard_map/cond/branch_0_fun/ppermute | solution.py:44
  48.5 2.8 %collective-permute-start.2 = (bf16[8,5,2,48,128]{4,3,2,1,0:T(8,128)(2,1)S(1)}, bf16[8,5,2,48,128]{4,3,2,1,0:T(8,128)(2,1)S(1)}, u32[]{:S(2)}, u32[]{:S(2)}) collective-permute-start(bf16[8,5,2,48,128]{4,3,2,1,0:T(8,128)(2,1)S(1)} %branch_0_fun.4), channel_id=1, source_target_pairs={{0,8},{1,9},{2,10},{3,11},{4,12},{5,13},{6,14},{7,15},{8,0},{9,1},... | collective-permute-start | bytes 2949128 | tf_op jit(solution)/shard_map/cond/branch_0_fun/ppermute | solution.py:44
  51.3 12.0 %collective-permute-done.3.refs_3_ = bf16[8,5,2,48,128]{4,3,2,1,0:T(8,128)(2,1)S(1)} collective-permute-done((bf16[8,5,2,48,128]{4,3,2,1,0:T(8,128)(2,1)S(1)}, bf16[8,5,2,48,128]{4,3,2,1,0:T(8,128)(2,1)S(1)}, u32[]{:S(2)}, u32[]{:S(2)}) %collective-permute-start.3) | collective-permute-done | bytes 983072 | tf_op jit(solution)/shard_map/cond/branch_0_fun/ppermute | solution.py:44
  63.3 1.2 collective-permute-done.2.refs_2_
  64.5 0.6 all-to-all-done.refs_0_
  65.1 11.2 %branch_0_fun.5 = (bf16[8,3,1,48,128]{4,3,2,1,0:T(8,128)(2,1)S(1)}, bf16[8,3,2,48,128]{4,3,2,1,0:T(8,128)(2,1)S(1)}, bf16[8,5,2,48,128]{4,3,2,1,0:T(8,128)(2,1)S...) custom-call(s32[3,9]{1,0:T(4,128)S(1)} %get-tuple-element.18.valid, ...), custom_call_target="tpu_custom_call" | custom-call | flops 2831155200 | bytes 8388608 | tf_op jit(solution)/shard_map/cond/branch_0_fun/pallas_call | solution.py:226
  76.3 2.6 %collective-permute-start.4 = (bf16[8,5,2,48,128]{4,3,2,1,0:T(8,128)(2,1)S(1)}, bf16[8,5,2,48,128]{4,3,2,1,0:T(8,128)(2,1)S(1)}, u32[]{:S(2)}, u32[]{:S(2)}) collective-permute-start(bf16[8,5,2,48,128]{4,3,2,1,0:T(8,128)(2,1)S(1)} %get-tuple-element.29), channel_id=1, source_target_pairs={{0,8},{1,9},{2,10},{3,11},{4,12},{5,13},{6,14},{7,15},{8,0},{9,1},... | collective-permute-start | bytes 2949128 | tf_op jit(solution)/shard_map/cond/branch_0_fun/ppermute | solution.py:44
  78.9 3.4 %collective-permute-start.5 = (bf16[8,5,2,48,128]{4,3,2,1,0:T(8,128)(2,1)S(1)}, bf16[8,5,2,48,128]{4,3,2,1,0:T(8,128)(2,1)S(1)}, u32[]{:S(2)}, u32[]{:S(2)}) collective-permute-start(bf16[8,5,2,48,128]{4,3,2,1,0:T(8,128)(2,1)S(1)} %get-tuple-element.30), channel_id=1, source_target_pairs={{8,16},{9,17},{10,18},{11,19},{12,20},{13,21},{14,22},{15,23},{16,... | collective-permute-start | bytes 2949128 | tf_op jit(solution)/shard_map/cond/branch_0_fun/ppermute | solution.py:44
  82.3 10.0 %collective-permute-done.4.refs_2_.refs_0_ = bf16[8,5,2,48,128]{4,3,2,1,0:T(8,128)(2,1)S(1)} collective-permute-done((bf16[8,5,2,48,128]{4,3,2,1,0:T(8,128)(2,1)S(1)}, bf16[8,5,2,48,128]{4,3,2,1,0:T(8,128)(2,1)S(1)}, u32[]{:S(2)}, u32[]{:S(2)}) %collective-permute-start.4) | collective-permute-done | bytes 983072 | tf_op jit(solution)/shard_map/cond/branch_0_fun/ppermute | solution.py:44
  92.3 3.8 %collective-permute-done.5.refs_3_.refs_1_ = bf16[8,5,2,48,128]{4,3,2,1,0:T(8,128)(2,1)S(1)} collective-permute-done((bf16[8,5,2,48,128]{4,3,2,1,0:T(8,128)(2,1)S(1)}, bf16[8,5,2,48,128]{4,3,2,1,0:T(8,128)(2,1)S(1)}, u32[]{:S(2)}, u32[]{:S(2)}) %collective-permute-start.5) | collective-permute-done | bytes 983072 | tf_op jit(solution)/shard_map/cond/branch_0_fun/ppermute | solution.py:44
  96.1 0.8 branch_0_fun.6
  96.8 1.9 %collective-permute-start.6 = (bf16[8,1,2,48,128]{4,3,2,1,0:T(8,128)(2,1)S(1)}, bf16[8,1,2,48,128]{4,3,2,1,0:T(8,128)(2,1)S(1)}, u32[]{:S(2)}, u32[]{:S(2)}) collective-permute-start(bf16[8,1,2,48,128]{4,3,2,1,0:T(8,128)(2,1)S(1)} %get-tuple-element.33), channel_id=1, source_target_pairs={{0,1},{1,0},{2,3},{3,2},{4,5},{5,4},{6,7},{7,6},{8,9},{9,8},{10,11... | collective-permute-start | bytes 589832 | tf_op jit(solution)/shard_map/cond/branch_0_fun/ppermute | solution.py:44
  98.7 5.5 %collective-permute-start.7 = (bf16[8,1,2,48,128]{4,3,2,1,0:T(8,128)(2,1)S(1)}, bf16[8,1,2,48,128]{4,3,2,1,0:T(8,128)(2,1)S(1)}, u32[]{:S(2)}, u32[]{:S(2)}) collective-permute-start(bf16[8,1,2,48,128]{4,3,2,1,0:T(8,128)(2,1)S(1)} %get-tuple-element.34), channel_id=1, source_target_pairs={{1,2},{2,1},{3,4},{4,3},{5,6},{6,5},{9,10},{10,9},{11,12},{12,11},... | collective-permute-start | bytes 589832 | tf_op jit(solution)/shard_map/cond/branch_0_fun/ppermute | solution.py:44
  104.3 0.1 collective-permute-done.6.refs_2_
  104.4 3.5 %collective-permute-done.7.refs_3_ = bf16[8,1,2,48,128]{4,3,2,1,0:T(8,128)(2,1)S(1)} collective-permute-done((bf16[8,1,2,48,128]{4,3,2,1,0:T(8,128)(2,1)S(1)}, bf16[8,1,2,48,128]{4,3,2,1,0:T(8,128)(2,1)S(1)}, u32[]{:S(2)}, u32[]{:S(2)}) %collective-permute-start.7) | collective-permute-done | bytes 196640 | tf_op jit(solution)/shard_map/cond/branch_0_fun/ppermute | solution.py:44
  107.9 0.9 branch_0_fun.7
  109.1 0.0 copy-start.3
  109.1 34.1 %all_to_all.24.packed = bf16[8,3,3,48,128]{4,3,2,1,0:T(8,128)(2,1)S(1)} all-to-all(bf16[8,3,3,48,128]{4,3,2,1,0:T(8,128)(2,1)S(1)} %get-tuple-element.78), channel_id=1, replica_groups=mesh['ta'=8,'ha'=8,'wa'=8] {'ta'}, dimensions={0} | all-to-all | bytes 1769472 | tf_op jit(solution)/shard_map/all_to_all | solution.py:326
  143.2 1.7 %shard_map.78 = (bf16[48,3072]{1,0:T(8,128)(2,1)}, bf16[48,3072]{1,0:T(8,128)(2,1)}, bf16[48,3072]{1,0:T(8,128)(2,1)}) custom-call(s32[24]{0:T(128)S(1)} %copy-done.3, bf16[8,3,3,48,128]{4,3,2,1,0:T(8,128)(2,1)S(1)} %all_to_all.24.packed), custom_call_target="tpu_custom_call" | custom-call | tf_op jit(solution)/shard_map/pallas_call | solution.py:58
  (7 shorter events, 0.0 us)
Async XLA Ops:
  0.6 15.2 %copy-start.1 = (bf16[1,1,48,3072]{3,2,1,0:T(8,128)(2,1)S(1)}, bf16[1,1,48,3072]{3,2,1,0:T(8,128)(2,1)}, u32[]{:S(2)}) copy-start(bf16[1,1,48,3072]{3,2,1,0:T(8,128)(2,1)} %param.11) | copy-start | bytes 884740
  0.6 15.2 %copy-start = (bf16[1,1,48,3072]{3,2,1,0:T(8,128)(2,1)S(1)}, bf16[1,1,48,3072]{3,2,1,0:T(8,128)(2,1)}, u32[]{:S(2)}) copy-start(bf16[1,1,48,3072]{3,2,1,0:T(8,128)(2,1)} %param.8) | copy-start | bytes 884740
  4.8 30.1 %all-to-all-start.3 = ((bf16[8,3,2,48,128]{4,3,2,1,0:T(8,128)(2,1)}), bf16[8,3,2,48,128]{4,3,2,1,0:T(8,128)(2,1)S(1)}, u32[]{:S(2)}, u32[]{:S(2)}) async-start(bf16[8,3,2,48,128]{4,3,2,1,0:T(8,128)(2,1)} %get-tuple-element.73), calls=%async_computation.3 | async-start | bytes 1179648 | tf_op jit(solution)/shard_map/all_to_all | solution.py:326
  15.8 0.7 copy-start.2
  35.0 7.6 %collective-permute-start = (bf16[8,1,2,48,128]{4,3,2,1,0:T(8,128)(2,1)S(1)}, bf16[8,1,2,48,128]{4,3,2,1,0:T(8,128)(2,1)S(1)}, u32[]{:S(2)}, u32[]{:S(2)}) collective-permute-start(bf16[8,1,2,48,128]{4,3,2,1,0:T(8,128)(2,1)S(1)} %slice.4), channel_id=1, source_target_pairs={{0,1},{1,0},{2,3},{3,2},{4,5},{5,4},{6,7},{7,6},{8,9},{9,8},{10,11... | collective-permute-start | bytes 589832 | tf_op jit(solution)/shard_map/cond/branch_0_fun/ppermute | solution.py:44
  37.4 8.7 %collective-permute-start.1 = (bf16[8,1,2,48,128]{4,3,2,1,0:T(8,128)(2,1)S(1)}, bf16[8,1,2,48,128]{4,3,2,1,0:T(8,128)(2,1)S(1)}, u32[]{:S(2)}, u32[]{:S(2)}) collective-permute-start(bf16[8,1,2,48,128]{4,3,2,1,0:T(8,128)(2,1)S(1)} %slice.4), channel_id=1, source_target_pairs={{1,2},{2,1},{3,4},{4,3},{5,6},{6,5},{9,10},{10,9},{11,12},{12,11},... | collective-permute-start | bytes 589832 | tf_op jit(solution)/shard_map/cond/branch_0_fun/ppermute | solution.py:44
  42.5 22.6 %all-to-all-start = ((bf16[8,3,2,48,128]{4,3,2,1,0:T(8,128)(2,1)}), bf16[8,3,2,48,128]{4,3,2,1,0:T(8,128)(2,1)S(1)}, u32[]{:S(2)}, u32[]{:S(2)}) async-start(bf16[8,3,2,48,128]{4,3,2,1,0:T(8,128)(2,1)} %get-tuple-element.25), calls=%async_computation | async-start | bytes 1179648 | tf_op jit(solution)/shard_map/cond/branch_0_fun/all_to_all | solution.py:326
  46.1 17.2 %collective-permute-start.3 = (bf16[8,5,2,48,128]{4,3,2,1,0:T(8,128)(2,1)S(1)}, bf16[8,5,2,48,128]{4,3,2,1,0:T(8,128)(2,1)S(1)}, u32[]{:S(2)}, u32[]{:S(2)}) collective-permute-start(bf16[8,5,2,48,128]{4,3,2,1,0:T(8,128)(2,1)S(1)} %branch_0_fun.4), channel_id=1, source_target_pairs={{8,16},{9,17},{10,18},{11,19},{12,20},{13,21},{14,22},{15,23},{16,... | collective-permute-start | bytes 2949128 | tf_op jit(solution)/shard_map/cond/branch_0_fun/ppermute | solution.py:44
  48.5 16.0 %collective-permute-start.2 = (bf16[8,5,2,48,128]{4,3,2,1,0:T(8,128)(2,1)S(1)}, bf16[8,5,2,48,128]{4,3,2,1,0:T(8,128)(2,1)S(1)}, u32[]{:S(2)}, u32[]{:S(2)}) collective-permute-start(bf16[8,5,2,48,128]{4,3,2,1,0:T(8,128)(2,1)S(1)} %branch_0_fun.4), channel_id=1, source_target_pairs={{0,8},{1,9},{2,10},{3,11},{4,12},{5,13},{6,14},{7,15},{8,0},{9,1},... | collective-permute-start | bytes 2949128 | tf_op jit(solution)/shard_map/cond/branch_0_fun/ppermute | solution.py:44
  76.3 16.0 %collective-permute-start.4 = (bf16[8,5,2,48,128]{4,3,2,1,0:T(8,128)(2,1)S(1)}, bf16[8,5,2,48,128]{4,3,2,1,0:T(8,128)(2,1)S(1)}, u32[]{:S(2)}, u32[]{:S(2)}) collective-permute-start(bf16[8,5,2,48,128]{4,3,2,1,0:T(8,128)(2,1)S(1)} %get-tuple-element.29), channel_id=1, source_target_pairs={{0,8},{1,9},{2,10},{3,11},{4,12},{5,13},{6,14},{7,15},{8,0},{9,1},... | collective-permute-start | bytes 2949128 | tf_op jit(solution)/shard_map/cond/branch_0_fun/ppermute | solution.py:44
  78.9 17.2 %collective-permute-start.5 = (bf16[8,5,2,48,128]{4,3,2,1,0:T(8,128)(2,1)S(1)}, bf16[8,5,2,48,128]{4,3,2,1,0:T(8,128)(2,1)S(1)}, u32[]{:S(2)}, u32[]{:S(2)}) collective-permute-start(bf16[8,5,2,48,128]{4,3,2,1,0:T(8,128)(2,1)S(1)} %get-tuple-element.30), channel_id=1, source_target_pairs={{8,16},{9,17},{10,18},{11,19},{12,20},{13,21},{14,22},{15,23},{16,... | collective-permute-start | bytes 2949128 | tf_op jit(solution)/shard_map/cond/branch_0_fun/ppermute | solution.py:44
  96.8 7.6 %collective-permute-start.6 = (bf16[8,1,2,48,128]{4,3,2,1,0:T(8,128)(2,1)S(1)}, bf16[8,1,2,48,128]{4,3,2,1,0:T(8,128)(2,1)S(1)}, u32[]{:S(2)}, u32[]{:S(2)}) collective-permute-start(bf16[8,1,2,48,128]{4,3,2,1,0:T(8,128)(2,1)S(1)} %get-tuple-element.33), channel_id=1, source_target_pairs={{0,1},{1,0},{2,3},{3,2},{4,5},{5,4},{6,7},{7,6},{8,9},{9,8},{10,11... | collective-permute-start | bytes 589832 | tf_op jit(solution)/shard_map/cond/branch_0_fun/ppermute | solution.py:44
  98.7 9.1 %collective-permute-start.7 = (bf16[8,1,2,48,128]{4,3,2,1,0:T(8,128)(2,1)S(1)}, bf16[8,1,2,48,128]{4,3,2,1,0:T(8,128)(2,1)S(1)}, u32[]{:S(2)}, u32[]{:S(2)}) collective-permute-start(bf16[8,1,2,48,128]{4,3,2,1,0:T(8,128)(2,1)S(1)} %get-tuple-element.34), channel_id=1, source_target_pairs={{1,2},{2,1},{3,4},{4,3},{5,6},{6,5},{9,10},{10,9},{11,12},{12,11},... | collective-permute-start | bytes 589832 | tf_op jit(solution)/shard_map/cond/branch_0_fun/ppermute | solution.py:44
  109.1 34.1 %copy-start.3 = (s32[24]{0:T(128)S(1)}, s32[24]{0:T(128)}, u32[]{:S(2)}) copy-start(s32[24]{0:T(128)} %get-tuple-element.71.order) | copy-start | bytes 292
